TPU v7x, 32 devices: a whole 2x2x4 slice. The times are simulated.
32 devices in a mesh: fibre: 8 (over y, x, core), win: 4 (over z).
Axes of the slice: x: 2, y: 2, z: 4, core: 2. Of those that a mesh axis runs over, the one named last changes fastest.
Arguments:
- strain: bfloat16 [1024, 4, 2048], P('fibre', 'win'), may hold values from -6 to 6
- kernel: bfloat16 [31, 9], replicated, may hold values from -0.375 to 0.375
- plan: int32 [4], replicated, may hold values from 0 to 7
Outputs:
- stacks: bfloat16 [4, 256, 2, 128, 1024], P(None, 'win', None, None, 'fibre')
Inputs may be any that keep to these rules, and one draw needn't show every extreme that they name: `plan`: each step's entry is an index along fibre; entries may repeat.
All inputs are finite; a program needn't handle non-finite values.
Results may differ from a plain program's by a relative error of at most 0.0057.
Values may be sent and summed in bfloat16 or wider, within the bound.
A program may use at most 128 MiB of HBM per device.

v0:
```python
import math

import jax
import jax.numpy as jnp
from jax import lax
from jax.sharding import PartitionSpec as P

FB = 256
FLO = 8
BLK = 64
STEPS = 4


def with_halo(block, sides, width):
    for axis, dim in sides:
        count = lax.axis_size(axis)
        forward = [(i, i + 1) for i in range(count - 1)]
        backward = [(target, source) for source, target in forward]
        low = lax.ppermute(
            lax.slice_in_dim(block, block.shape[dim] - width, None, axis=dim), axis, forward
        )
        high = lax.ppermute(lax.slice_in_dim(block, 0, width, axis=dim), axis, backward)
        block = jnp.concatenate([low, block, high], axis=dim)
    return block


def spectrum_table(samples, first_bin, bin_count):
    sample_index = jnp.arange(samples, dtype=jnp.int32)
    bin_index = first_bin + jnp.arange(bin_count, dtype=jnp.int32)
    phase_index = sample_index[:, None] * bin_index[None, :] % samples
    angles = phase_index.astype(jnp.float32) * (2.0 * math.pi / samples)
    return jnp.concatenate([jnp.cos(angles), -jnp.sin(angles)], axis=1)


def filter_block(padded, kernel):
    chan_taps = kernel.shape[0]
    time_taps = kernel.shape[1]
    half_time = time_taps // 2
    padded_rows = padded.shape[0]
    own_channels = padded_rows - (chan_taps - 1)
    samples = padded.shape[2]
    offsets = (
        jnp.arange(padded_rows, dtype=jnp.int32)[None, :]
        - jnp.arange(own_channels, dtype=jnp.int32)[:, None]
    )
    picks = (offsets[None, :, :] == jnp.arange(chan_taps, dtype=jnp.int32)[:, None, None]).astype(
        jnp.float32
    )
    band = jnp.einsum(
        "aij,ab->bij", picks, kernel.astype(jnp.float32), precision=lax.Precision.HIGHEST
    ).astype(jnp.bfloat16)
    by_window = jnp.transpose(padded, (1, 0, 2))

    def one_window(records):
        timed = jnp.pad(records, ((0, 0), (half_time, half_time)))
        shifted = jnp.stack([timed[:, offset : offset + samples] for offset in range(time_taps)])
        return lax.dot_general(
            band, shifted, (((0, 2), (0, 1)), ((), ())), preferred_element_type=jnp.float32
        )

    result = lax.map(one_window, by_window)
    return jnp.transpose(result, (1, 0, 2))


def whiten(spectra, bin_block):
    half_width = spectra.shape[-1] // 2
    real_part = spectra[..., :half_width]
    imag_part = spectra[..., half_width:]
    magnitude = jnp.sqrt(real_part * real_part + imag_part * imag_part)
    grouped = magnitude.reshape(magnitude.shape[:-1] + (half_width // bin_block, bin_block))
    amp_level = jnp.mean(grouped, axis=-1) + 1e-06
    factor = jnp.repeat(1.0 / amp_level, bin_block, axis=-1)
    stacked = jnp.stack([real_part * factor, imag_part * factor])
    return jnp.transpose(stacked, (0, 2, 3, 1)).astype(jnp.bfloat16)


def correlate(source, receivers, stack_scale):
    swapped = jnp.stack([receivers[1], -receivers[0]])
    numbers = (((0, 1), (0, 1)), ((2,), (2,)))
    real_sum = lax.dot_general(source, receivers, numbers, preferred_element_type=jnp.float32)
    imag_sum = lax.dot_general(source, swapped, numbers, preferred_element_type=jnp.float32)
    return (jnp.stack([real_sum, imag_sum], axis=1) * stack_scale).astype(jnp.bfloat16)


def shards(strain, kernel, plan):
    margin = kernel.shape[0] // 2
    padded = with_halo(strain, (("fibre", 0),), margin)
    filtered = filter_block(padded, kernel)
    basis_table = spectrum_table(strain.shape[2], FLO, FB)
    spectra = jnp.dot(
        filtered, basis_table, precision=lax.Precision.HIGHEST, preferred_element_type=jnp.float32
    )
    whitened = whiten(spectra, BLK)
    receivers = lax.all_to_all(whitened, "win", split_axis=2, concat_axis=1, tiled=True)
    stack_scale = 1.0 / math.sqrt(receivers.shape[1])
    block_width = receivers.shape[3]
    outputs = []
    everyone = lax.all_gather(receivers, "fibre", axis=3, tiled=True)
    for step_index in range(STEPS):
        first_channel = plan[step_index] * block_width
        source = lax.dynamic_slice_in_dim(everyone, first_channel, block_width, 3)
        outputs.append(correlate(source, receivers, stack_scale))
    return jnp.stack(outputs)


def solution(mesh):
    placed = (P("fibre", "win", None), P(), P())
    return jax.shard_map(
        shards,
        mesh=mesh,
        in_specs=placed,
        out_specs=P(None, "win", None, None, "fibre"),
        check_vma=False,
    )
```

profile of v0, /device:TPU:0, one launch (start us, length us, event | category | flops | bytes accessed | tf_op | source)
XLA Modules:
  0.0 103.5 jit_solution(7080628373060128857)
XLA Ops:
  6.5 0.0 copy-start
  6.5 0.0 all-gather.2.cloned.1.call-start
  6.5 0.9 fusion.48
  7.5 2.4 %collective-permute-start = (bf16[15,1,2048]{2,0,1:T(8,128)(2,1)S(1)}, bf16[15,1,2048]{2,0,1:T(8,128)(2,1)S(1)}, u32[]{:S(2)}, u32[]{:S(2)}) collective-permute-start(bf16[15,1,2048]{2,0,1:T(8,128)(2,1)S(1)} %get-tuple-element.11), channel_id=1, source_target_pairs={{0,4},{4,8},{8,12},{12,16},{16,20},{20,24},{24,28},{1,5},{5,9},{9,... | collective-permute-start | bytes 184328 | tf_op jit(solution)/shard_map/ppermute | solution.py:19
  9.9 1.3 %collective-permute-start.1 = (bf16[15,1,2048]{2,0,1:T(8,128)(2,1)S(1)}, bf16[15,1,2048]{2,0,1:T(8,128)(2,1)S(1)}, u32[]{:S(2)}, u32[]{:S(2)}) collective-permute-start(bf16[15,1,2048]{2,0,1:T(8,128)(2,1)S(1)} %get-tuple-element.16), channel_id=1, source_target_pairs={{4,0},{8,4},{12,8},{16,12},{20,16},{24,20},{28,24},{5,1},{9,5},{13... | collective-permute-start | bytes 184328 | tf_op jit(solution)/shard_map/ppermute | solution.py:22
  11.2 8.2 %fusion.21 = (f32[2048,256]{1,0:T(8,128)S(1)}, f32[2048,256]{1,0:T(8,128)S(1)}) fusion(s32[256]{0:T(256)S(1)} %iota_add_fusion), kind=kLoop, calls=%fused_computation.38 | loop fusion | flops 7864320 | bytes 4195328 | tf_op jit(solution)/shard_map/cos | solution.py:32
  19.4 0.0 copy-done
  19.4 1.0 fusion.17
  20.4 0.0 collective-permute-done
  20.4 0.0 collective-permute-done.1
  20.4 0.0 copy-done.2
  20.4 0.2 fusion.23
  20.6 0.3 bitcast_dynamic-update-slice_fusion.8
  20.9 0.3 bitcast_dynamic-update-slice_fusion.7
  21.2 0.3 bitcast_dynamic-update-slice_fusion.6
  21.4 0.3 bitcast_dynamic-update-slice_fusion.5
  21.7 0.2 bitcast_dynamic-update-slice_fusion.4
  21.9 0.3 bitcast_dynamic-update-slice_fusion.3
  22.2 0.3 bitcast_dynamic-update-slice_fusion.2
  22.4 0.3 bitcast_dynamic-update-slice_fusion.1
  22.7 0.3 bitcast_dynamic-update-slice_fusion
  22.9 1.5 %convolution_bitcast_fusion = f32[128,2048]{1,0:T(8,128)S(1)} fusion(bf16[9,158,2048]{2,1,0:T(8,128)(2,1)S(1)} %bitcast_dynamic-update-slice_fusion, bf16[9,128,158]{2,0,1:T(8,128)(2,1)S(1)} %fusion.17), kind=kOutput, calls=%fused_computation.18 | convolution fusion | flops 745537536 | bytes 7237120 | tf_op jit(solution)/shard_map/while/body/eval_jaxpr/dot_general | solution.py:57
  24.5 0.0 copy-start.4
  24.5 2.4 %fusion.18 = f32[128,1,512]{2,0,1:T(8,128)S(1)} fusion(f32[128,2048]{1,0:T(8,128)S(1)} %convolution_bitcast_fusion, f32[2048,256]{1,0:T(8,128)S(1)} %get-tuple-element.24, f32[2048,256]{1,0:T(8,128)S(1)} %get-tuple-element.23), kind=kOutput, calls=%fused_computation.37 | convolution fusion | flops 1611661312 | bytes 5505024 | tf_op jit(solution)/shard_map/dot_general | solution.py:90
  27.0 0.1 copy.43
  27.1 0.1 copy.44
  27.3 0.1 copy.46
  27.4 11.5 %all_to_all.12 = bf16[2,1,256,128]{3,0,1,2:T(2,128)(2,1)S(1)} all-to-all(bf16[2,1,256,128]{3,0,1,2:T(2,128)(2,1)S(1)} %copy.46), channel_id=1, replica_groups=mesh['fibre'=8,'win'=4] {'win'}, dimensions={2} | all-to-all | bytes 262144 | tf_op jit(solution)/shard_map/all_to_all | solution.py:94
  38.9 0.8 copy.48
  39.7 0.0 all-gather.2.cloned.1.call-update
  39.7 0.7 fusion.50
  43.0 0.2 fusion.49
  43.2 0.1 copy_dynamic-update-slice_fusion.1
  43.3 0.1 copy_dynamic-update-slice_fusion
  43.3 25.8 %all-gather.2.cloned.1.call-done = bf16[2,4,64,1024]{3,1,0,2:T(4,128)(2,1)} async-done(((bf16[2,4,64,128]{3,1,0,2:T(4,128)(2,1)}), bf16[2,4,64,1024]{3,1,0,2:T(4,128)(2,1)}) %all-gather.2.cloned.1.call-update) | async-done | bytes 1048592 | tf_op jit(solution)/shard_map/all_gather | solution.py:98
  69.1 1.8 %convolution_bitcast_fusion.2 = f32[1,64,1,128,128]{4,3,1,2,0:T(8,128)S(1)} fusion(bf16[2,4,64,1024]{3,1,0,2:T(4,128)(2,1)} %all-gather.2.cloned.1.call-done, s32[]{:T(128)S(6)} %select_n.25, bf16[2,4,64,128]{3,2,1,0:T(8,128)(2,1)S(1)} %bitcast.91), kind=kOutput, calls=%fused_computation.20 | convolution fusion | flops 16777216 | bytes 4456452 | tf_op jit(solution)/shard_map/dot_general | solution.py:80
  70.9 0.8 convolution_bitcast_fusion.1
  71.8 0.8 convolution_bitcast_fusion.3
  72.6 0.8 convolution_bitcast_fusion.4
  73.5 2.3 %fusion.2 = (bf16[1,64,2,128,128]{4,3,1,2,0:T(8,128)(2,1)S(1)}, bf16[1,64,2,128,128]{4,3,1,2,0:T(8,128)(2,1)S(1)}) fusion(f32[1,64,1,128,128]{4,3,1,2,0:T(8,128)S(1)} %convolution_bitcast_fusion.3, f32[1,64,1,128,128]{4,3,1,2,0:T(8,128)S(1)} %convolution_bitcast_fusion.4, f32[1,64,1,128,128]{4,3,1,2,0:T(8,128)S(1)} %convolution_bitcast_fusion.1, ...), kind=kLoop, calls=%fused_computation.6 | loop fusion | flops 12582912 | bytes 25165824 | tf_op jit(solution)/shard_map/convert_element_type | solution.py:82
  75.8 0.8 convolution_bitcast_fusion.7
  76.6 0.8 convolution_bitcast_fusion.8
  77.5 0.8 convolution_bitcast_fusion.5
  78.3 0.8 convolution_bitcast_fusion.6
  79.2 4.5 %fusion = (bf16[1,64,2,128,128]{4,3,1,2,0:T(8,128)(2,1)}, bf16[1,64,2,128,128]{4,3,1,2,0:T(8,128)(2,1)}) fusion(f32[1,64,1,128,128]{4,3,1,2,0:T(8,128)S(1)} %convolution_bitcast_fusion.7, f32[1,64,1,128,128]{4,3,1,2,0:T(8,128)S(1)} %convolution_bitcast_fusion.8, f32[1,64,1,128,128]{4,3,1,2,0:T(8,128)S(1)} %convolution_bitcast_fusion.5, ...), kind=kLoop, calls=%fused_computation.2 | loop fusion | flops 12582912 | bytes 25165824 | tf_op jit(solution)/shard_map/convert_element_type | solution.py:82
  83.7 6.4 %pad_maximum_fusion = bf16[4,64,2,128,128]{4,3,1,2,0:T(8,128)(2,1)S(1)} fusion(bf16[1,64,2,128,128]{4,3,1,2,0:T(8,128)(2,1)S(1)} %get-tuple-element.32, bf16[1,64,2,128,128]{4,3,1,2,0:T(8,128)(2,1)S(1)} %get-tuple-element.31, bf16[1,64,2,128,128]{4,3,1,2,0:T(8,128)(2,1)} %get-tuple-element.30, bf16[1,64,2,128,128]{4,3,1,2,0:T(8,128)(2,1)} %get-tuple-element.29), kind=kLoop, calls=%fused_computation | loop fusion | flops 25165824 | bytes 33554432 | tf_op jit(solution)/shard_map/stack | solution.py:103
  90.1 0.0 copy-start.1
  90.1 6.5 %copy.57 = bf16[4,64,2,128,128]{4,3,2,1,0:T(8,128)(2,1)} copy(bf16[4,64,2,128,128]{4,3,1,2,0:T(8,128)(2,1)S(1)} %pad_maximum_fusion) | data formatting | bytes 33554432 | tf_op jit(solution)/shard_map/stack | solution.py:103
  (16 shorter events, 0.2 us)
Async XLA Ops:
  6.5 12.9 %copy-start = (bf16[31,9]{0,1:T(8,128)(2,1)S(1)}, bf16[31,9]{0,1:T(8,128)(2,1)}, u32[]{:S(2)}) copy-start(bf16[31,9]{0,1:T(8,128)(2,1)} %param.4) | copy-start | bytes 1678
  6.5 13.9 %copy-start.2 = (bf16[128,1,2048]{2,0,1:T(8,128)(2,1)S(1)}, bf16[128,1,2048]{2,0,1:T(8,128)(2,1)}, u32[]{:S(2)}) copy-start(bf16[128,1,2048]{2,0,1:T(8,128)(2,1)} %param.3) | copy-start | bytes 1572868
  6.5 62.6 %all-gather.2.cloned.1.call-start = ((), (), s32[]{:S(2)}) async-start(), calls=%async_computation.1 | async-start | bytes 1179648 | tf_op jit(solution)/shard_map/all_gather | solution.py:98
  7.5 12.9 %collective-permute-start = (bf16[15,1,2048]{2,0,1:T(8,128)(2,1)S(1)}, bf16[15,1,2048]{2,0,1:T(8,128)(2,1)S(1)}, u32[]{:S(2)}, u32[]{:S(2)}) collective-permute-start(bf16[15,1,2048]{2,0,1:T(8,128)(2,1)S(1)} %get-tuple-element.11), channel_id=1, source_target_pairs={{0,4},{4,8},{8,12},{12,16},{16,20},{20,24},{24,28},{1,5},{5,9},{9,... | collective-permute-start | bytes 184328 | tf_op jit(solution)/shard_map/ppermute | solution.py:19
  9.9 10.6 %collective-permute-start.1 = (bf16[15,1,2048]{2,0,1:T(8,128)(2,1)S(1)}, bf16[15,1,2048]{2,0,1:T(8,128)(2,1)S(1)}, u32[]{:S(2)}, u32[]{:S(2)}) collective-permute-start(bf16[15,1,2048]{2,0,1:T(8,128)(2,1)S(1)} %get-tuple-element.16), channel_id=1, source_target_pairs={{4,0},{8,4},{12,8},{16,12},{20,16},{24,20},{28,24},{5,1},{9,5},{13... | collective-permute-start | bytes 184328 | tf_op jit(solution)/shard_map/ppermute | solution.py:22
  24.5 15.2 %copy-start.4 = (s32[4]{0:T(128)S(1)}, s32[4]{0:T(128)}, u32[]{:S(2)}) copy-start(s32[4]{0:T(128)} %param.5) | copy-start | bytes 52
  69.1 1.8 %copy-start.3 = (bf16[2,4,64,1024]{3,1,0,2:T(4,128)(2,1)S(1)}, bf16[2,4,64,1024]{3,1,0,2:T(4,128)(2,1)}, u32[]{:S(2)}) copy-start(bf16[2,4,64,1024]{3,1,0,2:T(4,128)(2,1)} %all-gather.2.cloned.1.call-done) | copy-start | bytes 3145732
  90.1 6.5 %copy-start.1 = (bf16[31,9]{0,1:T(8,128)(2,1)S(1)}, bf16[31,9]{0,1:T(8,128)(2,1)}, u32[]{:S(2)}) copy-start(bf16[31,9]{0,1:T(8,128)(2,1)} %param.4) | copy-start | bytes 1678
Sparse Core Ops, SparseCore 0:
  39.8 29.2 all-gather.1
where the time goes:
time: 104 us; the launch traced here: 103 us
  waiting for transfers between devices  25.8 us (25%)
  other arithmetic  22 us (21%)
  between operations  16.3 us (16%)
  matrix products  12.6 us (12%)
  local copies, waits for them, and re-layouts  11.6 us (11%)
  blocking collectives  11.5 us (11%)
  starting transfers between devices  3.65 us (4%)
    all_gather x1, waiting for transfers between devices, shards(): everyone = lax.all_gather(receivers, 'fibre', axis=3, tiled=True)  25.8 us
    all_to_all x1, blocking collectives, shards(): lax.all_to_all(whitened, 'win', split_axis=2, concat_axis=1, tiled=True)  11.5 us
    cos x1, other arithmetic, spectrum_table(): return jnp.concatenate([jnp.cos(angles), -jnp.sin(angles)], axis=1)  8.24 us
    convert_element_type x2, other arithmetic, correlate(): (jnp.stack([real_sum, imag_sum], axis=1) * stack_scale).astype(jnp.bfloat16)  6.82 us
    another operation x1, local copies, waits for them, and re-layouts, shards(): return jnp.stack(outputs)  6.53 us
    another operation x1, other arithmetic, shards(): return jnp.stack(outputs)  6.42 us
    dot_general x4, matrix products, correlate(): lax.dot_general(source, receivers, numbers, preferred_element_type=jnp.fl...  4.31 us
    dot_general x4, matrix products, correlate(): lax.dot_general(source, swapped, numbers, preferred_element_type=jnp.floa...  3.38 us
  transfers between devices with their start and end apart: 3, of which 1 were waited for; matrix products, arithmetic and copies ran while one was open for 10% of the time, Pallas kernels for 0%

commit v1 on v0

v1 whole, which is shorter than its diff:
```python
import functools
import math

import jax
import jax.numpy as jnp
import ml_dtypes
import numpy as np
from jax import lax
from jax.experimental import pallas as pl
from jax.experimental.pallas import tpu as pltpu
from jax.sharding import PartitionSpec as P

FB = 256
FLO = 8
BLK = 64
ROWS = 16
MESH = pl.DeviceIdType.MESH


def tap_order(half_time):
    order = [0]
    for offset in range(1, half_time + 1):
        order += [offset, -offset]
    return order


@functools.lru_cache(maxsize=None)
def transform_table(samples, bins, half_time):
    index = np.arange(samples, dtype=np.int64)
    blocks = []
    for start in range(0, FB, bins):
        wanted = FLO + start + np.arange(bins, dtype=np.int64)
        angles = (wanted[:, None] * index[None, :] % samples) * (2.0 * np.pi / samples)
        exact = np.concatenate([np.cos(angles), -np.sin(angles)])
        high = exact.astype(ml_dtypes.bfloat16)
        low = (exact - high.astype(np.float64)).astype(ml_dtypes.bfloat16)
        blocks += [high, low]
    picks = np.zeros((-(-2 * half_time // ROWS) * ROWS, samples), ml_dtypes.bfloat16)
    for row in range(half_time):
        picks[row, row] = 1
        picks[half_time + row, samples - half_time + row] = 1
    return np.concatenate(blocks + [picks])


@functools.lru_cache(maxsize=None)
def phase_table(samples, half_time):
    wanted = FLO + np.arange(FB, dtype=np.int64)
    angles = wanted[:, None] * np.arange(1, half_time + 1)[None, :] % samples * (2.0 * np.pi / samples)
    return np.concatenate([np.cos(angles), np.sin(angles)], axis=1).astype(np.float32)


def gather_orders(count):
    bits = [1 << place for place in range(1, count.bit_length() - 1)]
    return [bits + [1], bits[::-1] + [1]]


def spectra_kernel(
    fibres, wins, margin, half_time,
    taps_ref, phase_ref, table_ref, strain_ref, out_ref,
    table_v, x_v, d_v, band_v, white_v,
    load_sem, halo_send, halo_recv, swap_send, swap_recv, keep_sem, gather_send, gather_recv,
):
    me = lax.axis_index("fibre")
    win = lax.axis_index("win")
    channels = strain_ref.shape[0]
    bins = white_v.shape[2]
    halo = (x_v.shape[0] - channels) // 2
    chan_taps = 2 * margin + 1
    order = tap_order(half_time)

    load_table = pltpu.make_async_copy(table_ref, table_v, load_sem.at[0])
    load_table.start()
    load_own = pltpu.make_async_copy(strain_ref, x_v.at[pl.ds(0, channels)], load_sem.at[1])
    load_own.start()

    barrier = pltpu.get_barrier_semaphore()
    for step in range(1, fibres):
        pl.semaphore_signal(barrier, inc=1, device_id={"fibre": lax.rem(me + step, fibres)}, device_id_type=MESH)
    for step in range(1, wins):
        pl.semaphore_signal(barrier, inc=1, device_id={"win": lax.rem(win + step, wins)}, device_id_type=MESH)
    pl.semaphore_wait(barrier, fibres + wins - 2)

    to_right = pltpu.make_async_remote_copy(
        src_ref=strain_ref.at[pl.ds(channels - halo, halo)], dst_ref=x_v.at[pl.ds(channels, halo)],
        send_sem=halo_send.at[0], recv_sem=halo_recv.at[0],
        device_id={"fibre": lax.rem(me + 1, fibres)}, device_id_type=MESH,
    )
    to_left = pltpu.make_async_remote_copy(
        src_ref=strain_ref.at[pl.ds(0, halo)], dst_ref=x_v.at[pl.ds(channels + halo, halo)],
        send_sem=halo_send.at[1], recv_sem=halo_recv.at[1],
        device_id={"fibre": lax.rem(me + fibres - 1, fibres)}, device_id_type=MESH,
    )
    first, last = me == 0, me == fibres - 1

    @pl.when(jnp.logical_not(last))
    def _():
        to_right.start()

    @pl.when(jnp.logical_not(first))
    def _():
        to_left.start()

    @pl.when(first)
    def _():
        x_v[channels : channels + halo, :] = jnp.zeros((halo, x_v.shape[1]), x_v.dtype)

    @pl.when(last)
    def _():
        x_v[channels + halo :, :] = jnp.zeros((halo, x_v.shape[1]), x_v.dtype)

    for low, size, start in ((0, channels, 0), (channels, halo, -halo), (channels + halo, halo, channels)):
        for piece in range(0, size, 64):
            rows = min(64, size - piece)
            shape = (rows, channels)
            lag = (
                lax.broadcasted_iota(jnp.int32, shape, 0) + (start + piece + margin)
                - lax.broadcasted_iota(jnp.int32, shape, 1)
            )
            totals = [jnp.zeros(shape, jnp.float32)] * len(order)
            least = start + piece + margin - (channels - 1)
            most = start + piece + margin + rows - 1
            for tap in range(max(0, least), min(chan_taps - 1, most) + 1):
                here = lag == tap
                totals = [
                    jnp.where(here, taps_ref[tap, offset + half_time], total)
                    for total, offset in zip(totals, order)
                ]
            for place, total in enumerate(totals):
                band_v[low + piece : low + piece + rows, place * channels : (place + 1) * channels] = total.astype(
                    jnp.bfloat16
                )

    load_own.wait()

    @pl.when(jnp.logical_not(last))
    def _():
        to_right.wait_send()
        to_left.wait_recv()

    @pl.when(jnp.logical_not(first))
    def _():
        to_left.wait_send()
        to_right.wait_recv()

    load_table.wait()
    d_v[...] = lax.dot_general(
        table_v[...], x_v[...], (((1,), (1,)), ((), ())), preferred_element_type=jnp.float32
    )

    edges = d_v[4 * FB :, :].astype(jnp.bfloat16)
    tails = jnp.dot(edges, band_v[...], preferred_element_type=jnp.float32)

    def tail(row, offset):
        place = order.index(offset)
        return tails[row : row + 1, place * channels : (place + 1) * channels]

    before = {m: sum(tail(u, m + u) for u in range(half_time - m + 1)) for m in range(1, half_time + 1)}
    after = {
        m: sum(tail(2 * half_time - v, -(v + m)) for v in range(1, half_time - m + 1)) for m in range(half_time)
    }

    def whiten_group(group):
        base = pl.multiple_of(group * (4 * bins), 4 * bins)
        both = d_v[pl.ds(base, 2 * bins), :] + d_v[pl.ds(base + 2 * bins, 2 * bins), :]
        high = both.astype(jnp.bfloat16)
        low = (both - high.astype(jnp.float32)).astype(jnp.bfloat16)

        def banded(place, width):
            band = band_v[:, place * channels : (place + width) * channels]
            return jnp.dot(high, band, preferred_element_type=jnp.float32) + jnp.dot(
                low, band, preferred_element_type=jnp.float32
            )

        plain = banded(0, 1)
        real = plain[:bins] - after[0]
        imag = plain[bins:]
        bin_rows = pl.ds(pl.multiple_of(group * bins, bins), bins)
        for offset in range(1, half_time + 1):
            pair = banded(2 * offset - 1, 2)
            ahead_re = pair[:bins, :channels] - before[offset]
            back_re = pair[:bins, channels:]
            if offset in after:
                back_re = back_re - after[offset]
            ahead_im, back_im = pair[bins:, :channels], pair[bins:, channels:]
            cos = phase_ref[bin_rows, offset - 1 : offset]
            sin = phase_ref[bin_rows, half_time + offset - 1 : half_time + offset]
            real += cos * (ahead_re + back_re) - sin * (ahead_im - back_im)
            imag += cos * (ahead_im + back_im) + sin * (ahead_re - back_re)
        magnitude = jnp.sqrt(real * real + imag * imag)
        for start in range(0, bins, BLK):
            level = jnp.mean(magnitude[start : start + BLK], axis=0, keepdims=True) + 1e-06
            factor = 1.0 / level
            white_v[group, 0, start : start + BLK] = (real[start : start + BLK] * factor).astype(jnp.bfloat16)
            white_v[group, 1, start : start + BLK] = (imag[start : start + BLK] * factor).astype(jnp.bfloat16)

    def swap(step):
        target = lax.rem(win + step, wins)
        return pltpu.make_async_remote_copy(
            src_ref=white_v.at[target], dst_ref=out_ref.at[me, win],
            send_sem=swap_send.at[step], recv_sem=swap_recv.at[step],
            device_id={"win": target}, device_id_type=MESH,
        )

    def swap_arrival(step):
        source = lax.rem(win + wins - step, wins)
        return pltpu.make_async_remote_copy(
            src_ref=white_v.at[win], dst_ref=out_ref.at[me, source],
            send_sem=swap_send.at[step], recv_sem=swap_recv.at[step],
            device_id={"win": source}, device_id_type=MESH,
        )

    steps = sorted(range(1, wins), key=lambda step: -min(step, wins - step))
    for step in steps:
        whiten_group(lax.rem(win + step, wins))
        swap(step).start()
    whiten_group(win)
    keep = pltpu.make_async_copy(white_v.at[win], out_ref.at[me, win], keep_sem)
    keep.start()

    orders = gather_orders(fibres)
    arrival_order = [0] + sorted(range(1, wins), key=lambda step: min(step, wins - step))

    def hop(step, away, bit):
        block = lax.bitwise_xor(me, away)
        window = lax.rem(win + wins - step, wins)
        source = white_v.at[win] if step == 0 and away == 0 else out_ref.at[block, window]
        return pltpu.make_async_remote_copy(
            src_ref=source, dst_ref=out_ref.at[block, window],
            send_sem=gather_send.at[away ^ bit, step], recv_sem=gather_recv.at[away ^ bit, step],
            device_id={"fibre": lax.bitwise_xor(me, bit)}, device_id_type=MESH,
        )

    events = []
    for rank, step in enumerate(arrival_order):
        line = orders[rank % 2]
        for away in range(fibres):
            taken = [place for place, bit in enumerate(line) if away & bit]
            latest = max(taken, default=-1)
            events.append((rank + len(taken), rank, latest, away, step, line))
    events.sort(key=lambda event: event[:4])
    started = []
    for _, _, latest, away, step, line in events:
        if away:
            hop(step, away ^ line[latest], line[latest]).wait_recv()
        elif step:
            swap_arrival(step).wait_recv()
        for bit in line[latest + 1 :]:
            copy = hop(step, away, bit)
            copy.start()
            started.append(copy)
    keep.wait()
    for step in range(1, wins):
        swap(step).wait_send()
    for copy in started:
        copy.wait_send()


def stack_kernel(steps, scale, chosen_ref, *refs):
    sources, receiver, out_ref, left_v, right_v = refs[:steps], refs[steps], refs[steps + 1], refs[steps + 2], refs[steps + 3]
    wins, _, _, channels = receiver.shape[1:]
    depth = wins * 2 * ROWS
    per_step = out_ref.shape[1]
    first_bin = pl.program_id(0) * per_step
    exact = math.frexp(scale)[0] == 0.5

    @pl.when(first_bin % ROWS == 0)
    def _():
        group = pl.ds(pl.multiple_of(first_bin // ROWS * ROWS, ROWS), ROWS)
        for step, source in enumerate(sources):
            piece = source[0, :, :, group, :].reshape(depth, channels).astype(jnp.float32)
            if exact:
                piece = piece * scale
            left_v[step * channels : (step + 1) * channels, :] = piece.T.astype(jnp.bfloat16)
        real = receiver[0, :, 0, group, :]
        imag = receiver[0, :, 1, group, :]
        right_v[:, :channels] = jnp.stack([real, imag], axis=1).reshape(depth, channels)
        right_v[:, channels:] = jnp.stack([imag, -real], axis=1).reshape(depth, channels)

    row = lax.rem(lax.broadcasted_iota(jnp.int32, (depth, 2 * channels), 0), ROWS)
    for place in range(per_step):
        here = row == lax.rem(first_bin + place, ROWS)
        right = jnp.where(here, right_v[...].astype(jnp.float32), 0.0).astype(jnp.bfloat16)
        result = jnp.dot(left_v[...], right, preferred_element_type=jnp.float32)
        if not exact:
            result = result * scale
        result = result.astype(jnp.bfloat16)
        for step in range(steps):
            out_ref[step, place, 0] = result[step * channels : (step + 1) * channels, :channels]
            out_ref[step, place, 1] = result[step * channels : (step + 1) * channels, channels:]


def shards(strain, kernel, plan):
    fibres, wins = lax.axis_size("fibre"), lax.axis_size("win")
    channels, own_windows, samples = strain.shape
    margin, half_time = kernel.shape[0] // 2, kernel.shape[1] // 2
    bins = FB // wins
    halo = -(-margin // ROWS) * ROWS
    assert own_windows == 1 and bins % BLK == 0 and fibres & (fibres - 1) == 0
    table = transform_table(samples, bins, half_time)
    phases = phase_table(samples, half_time)
    any_space = pl.BlockSpec(memory_space=pl.ANY)
    gathered = pl.pallas_call(
        functools.partial(spectra_kernel, fibres, wins, margin, half_time),
        out_shape=jax.ShapeDtypeStruct((fibres, wins, 2, bins, channels), jnp.bfloat16),
        in_specs=[
            pl.BlockSpec(memory_space=pltpu.SMEM),
            pl.BlockSpec(memory_space=pltpu.VMEM),
            any_space,
            any_space,
        ],
        out_specs=any_space,
        scratch_shapes=[
            pltpu.VMEM(table.shape, jnp.bfloat16),
            pltpu.VMEM((channels + 2 * halo, samples), jnp.bfloat16),
            pltpu.VMEM((table.shape[0], channels + 2 * halo), jnp.float32),
            pltpu.VMEM((channels + 2 * halo, kernel.shape[1] * channels), jnp.bfloat16),
            pltpu.VMEM((wins, 2, bins, channels), jnp.bfloat16),
            pltpu.SemaphoreType.DMA((2,)),
            pltpu.SemaphoreType.DMA((2,)),
            pltpu.SemaphoreType.DMA((2,)),
            pltpu.SemaphoreType.DMA((wins,)),
            pltpu.SemaphoreType.DMA((wins,)),
            pltpu.SemaphoreType.DMA,
            pltpu.SemaphoreType.DMA((fibres, wins)),
            pltpu.SemaphoreType.DMA((fibres, wins)),
        ],
        compiler_params=pltpu.CompilerParams(
            collective_id=0, has_side_effects=True, vmem_limit_bytes=40 * 1024 * 1024
        ),
        name="spectra",
    )(kernel.astype(jnp.float32), jnp.asarray(phases), jnp.asarray(table), strain.reshape(channels, samples))

    steps = plan.shape[0]
    chosen = jnp.concatenate([plan, lax.axis_index("fibre").astype(plan.dtype)[None]])
    per_step = 4
    block = (1, wins, 2, bins, channels)

    def pick(place):
        return pl.BlockSpec(block, lambda i, chosen_ref: (chosen_ref[place], 0, 0, 0, 0))

    return pl.pallas_call(
        functools.partial(stack_kernel, steps, 1.0 / math.sqrt(wins * own_windows)),
        out_shape=jax.ShapeDtypeStruct((steps, bins, 2, channels, channels), jnp.bfloat16),
        grid_spec=pltpu.PrefetchScalarGridSpec(
            num_scalar_prefetch=1,
            grid=(bins // per_step,),
            in_specs=[pick(place) for place in range(steps + 1)],
            out_specs=pl.BlockSpec((steps, per_step, 2, channels, channels), lambda i, chosen_ref: (0, i, 0, 0, 0)),
            scratch_shapes=[
                pltpu.VMEM((steps * channels, wins * 2 * ROWS), jnp.bfloat16),
                pltpu.VMEM((wins * 2 * ROWS, 2 * channels), jnp.bfloat16),
            ],
        ),
        compiler_params=pltpu.CompilerParams(vmem_limit_bytes=40 * 1024 * 1024),
        name="stacks",
    )(chosen, *([gathered] * (steps + 1)))


def solution(mesh):
    placed = (P("fibre", "win", None), P(), P())
    return jax.shard_map(
        shards,
        mesh=mesh,
        in_specs=placed,
        out_specs=P(None, "win", None, None, "fibre"),
        check_vma=False,
    )
```

time: 104 us -> 49.5 us (0.48)
  Pallas kernels: 0 us -> 43.5 us
  waiting for transfers between devices: 25.8 us -> 0 us
  other arithmetic: 22 us -> 0.73 us
  between operations: 16.3 us -> 0.01 us
  matrix products: 12.6 us -> 0 us
  blocking collectives: 11.5 us -> 0 us
  local copies, waits for them, and re-layouts: 11.6 us -> 4.93 us
  starting transfers between devices: 3.65 us -> 0 us
    pallas_call x0 -> x2, Pallas kernels: none -> 43.5 us  [the longest x1 30.9 us: shards(): pl.pallas_call(functools.partial(spectra_kernel, fibres, wins, margin, ha...]
    all_gather x1 -> x0, waiting for transfers between devices: 25.8 us -> none  [shards(): everyone = lax.all_gather(receivers, 'fibre', axis=3, tiled=True)]
    dot_general x11 -> x0, matrix products: 12.6 us -> none  [the longest x4 4.31 us: correlate(): lax.dot_general(source, receivers, numbers, preferred_element_type=jnp.fl...]
    all_to_all x1 -> x0, blocking collectives: 11.5 us -> none  [shards(): lax.all_to_all(whitened, 'win', split_axis=2, concat_axis=1, tiled=True)]
    cos x1 -> x0, other arithmetic: 8.24 us -> none  [spectrum_table(): return jnp.concatenate([jnp.cos(angles), -jnp.sin(angles)], axis=1)]
    another operation x3 -> x0, local copies, waits for them, and re-layouts: 6.86 us -> none  [the longest x1 6.53 us: shards(): return jnp.stack(outputs)]
    convert_element_type x3 -> x0, other arithmetic: 6.83 us -> none  [the longest x2 6.82 us: correlate(): (jnp.stack([real_sum, imag_sum], axis=1) * stack_scale).astype(jnp.bfloat16)]
    another operation x2 -> x0, other arithmetic: 6.44 us -> none  [the longest x1 6.42 us: shards(): return jnp.stack(outputs)]
  transfers between devices with their start and end apart: 3 -> 0, of which waited for: 1 -> 0; matrix products, arithmetic and copies ran while one was open for 10% -> 0% of each run, Pallas kernels for 0% -> 0%
where the time goes in v1:
time: 49.5 us; the launch traced here: 49.2 us
  Pallas kernels  43.5 us (88%)
  local copies, waits for them, and re-layouts  4.93 us (10%)
  other arithmetic  0.73 us (1%)
    pallas_call x1, Pallas kernels, shards(): pl.pallas_call(functools.partial(spectra_kernel, fibres, wins, margin, ha...  30.9 us
    pallas_call x1, Pallas kernels, shards(): pl.pallas_call(functools.partial(stack_kernel, steps, 1.0 / math.sqrt(win...  12.7 us
    unnamed x6, local copies, waits for them, and re-layouts  4.15 us

profile of v1, /device:TPU:0, one launch (start us, length us, event | category | flops | bytes accessed | tf_op | source)
XLA Modules:
  0.0 49.2 jit_solution(3327745489618303096)
XLA Ops:
  0.0 0.7 %pad_add_fusion.chosen_ref = s32[5]{0:T(128)S(1)} fusion(s32[1]{0:T(128)} %bitcast, s32[4]{0:T(128)} %param.7), kind=kLoop, calls=%fused_computation | loop fusion | flops 5 | bytes 40 | tf_op jit(solution)/shard_map/concatenate | solution.py:334
  0.7 0.8 %copy.7.taps_ref = f32[31,9]{1,0:T(8,128)S(1)} copy(bf16[31,9]{0,1:T(8,128)(2,1)} %param.6) | data formatting | bytes 1674 | tf_op jit(solution)/shard_map/convert_element_type | solution.py:331
  1.5 0.0 copy-start
  1.5 2.2 %copy-done = bf16[1040,2048]{1,0:T(8,128)(2,1)S(1)} copy-done((bf16[1040,2048]{1,0:T(8,128)(2,1)S(1)}, bf16[1040,2048]{1,0:T(8,128)(2,1)}, u32[]{:S(2)}) %copy-start) | copy-done | bytes 4259864
  3.7 0.0 copy-start.1
  3.7 1.0 %copy-done.1 = bf16[128,1,2048]{2,0,1:T(8,128)(2,1)S(1)} copy-done((bf16[128,1,2048]{2,0,1:T(8,128)(2,1)S(1)}, bf16[128,1,2048]{2,0,1:T(8,128)(2,1)}, u32[]{:S(2)}) %copy-start.1) | copy-done | bytes 524312
  4.8 0.0 copy-start.2
  4.8 0.9 %copy-done.2 = f32[256,8]{1,0:T(8,128)S(1)} copy-done((f32[256,8]{1,0:T(8,128)S(1)}, f32[256,8]{1,0:T(8,128)}, u32[]{:S(2)}) %copy-start.2) | copy-done | bytes 8216
  5.7 30.9 %spectra.1.refs_0_.refs_1_.refs_2_.refs_3_.refs_4_ = bf16[8,4,2,64,128]{4,3,2,1,0:T(8,128)(2,1)S(1)} custom-call(f32[31,9]{1,0:T(8,128)S(1)} %copy.7.taps_ref, f32[256,8]{1,0:T(8,128)S(1)} %copy-done.2, bf16[1040,2048]{1,0:T(8,128)(2,1)S(1)} %copy-done, bf16[128,2048]{1,0:T(8,128)(2,1)S(1)} %bitcast.2), custom_call_target="tpu_custom_call" | custom-call | tf_op jit(solution)/shard_map/spectra/pallas_call | solution.py:302
  36.5 12.7 %stacks.1 = bf16[4,64,2,128,128]{4,3,2,1,0:T(8,128)(2,1)} custom-call(s32[5]{0:T(128)S(1)} %pad_add_fusion.chosen_ref, bf16[8,4,2,64,128]{4,3,2,1,0:T(8,128)(2,1)S(1)} %spectra.1.refs_0_.refs_1_.refs_2_.refs_3_.refs_4_, bf16[8,4,2,64,128]{4,3,2,1,0:T(8,128)(2,1)S(1)} %spectra.1.refs_0_.refs_1_.refs_2_.refs_3_.refs_4_, ...), custom_call_target="tpu_custom_call" | custom-call | tf_op jit(solution)/shard_map/stacks/pallas_call | solution.py:341
Async XLA Ops:
  1.5 2.2 %copy-start = (bf16[1040,2048]{1,0:T(8,128)(2,1)S(1)}, bf16[1040,2048]{1,0:T(8,128)(2,1)}, u32[]{:S(2)}) copy-start(bf16[1040,2048]{1,0:T(8,128)(2,1)} %constant.11.clone.table_ref) | copy-start | bytes 12779524
  3.7 1.0 %copy-start.1 = (bf16[128,1,2048]{2,0,1:T(8,128)(2,1)S(1)}, bf16[128,1,2048]{2,0,1:T(8,128)(2,1)}, u32[]{:S(2)}) copy-start(bf16[128,1,2048]{2,0,1:T(8,128)(2,1)} %param.5) | copy-start | bytes 1572868
  4.8 0.9 %copy-start.2 = (f32[256,8]{1,0:T(8,128)S(1)}, f32[256,8]{1,0:T(8,128)}, u32[]{:S(2)}) copy-start(f32[256,8]{1,0:T(8,128)} %constant.10.clone.phase_ref) | copy-start | bytes 24580

commit v2 on v1

--- a/solution.py
+++ b/solution.py
@@ -56,8 +56,8 @@
 
 def spectra_kernel(
     fibres, wins, margin, half_time,
-    taps_ref, phase_ref, table_ref, strain_ref, out_ref,
-    table_v, x_v, d_v, band_v, white_v,
+    taps_ref, phase_hbm, table_ref, strain_ref, out_ref,
+    phase_ref, table_v, x_v, d_v, band_v, white_v,
     load_sem, halo_send, halo_recv, swap_send, swap_recv, keep_sem, gather_send, gather_recv,
 ):
     me = lax.axis_index("fibre")
@@ -72,41 +72,14 @@
     load_table.start()
     load_own = pltpu.make_async_copy(strain_ref, x_v.at[pl.ds(0, channels)], load_sem.at[1])
     load_own.start()
+    load_phase = pltpu.make_async_copy(phase_hbm, phase_ref, load_sem.at[2])
+    load_phase.start()
 
     barrier = pltpu.get_barrier_semaphore()
     for step in range(1, fibres):
         pl.semaphore_signal(barrier, inc=1, device_id={"fibre": lax.rem(me + step, fibres)}, device_id_type=MESH)
     for step in range(1, wins):
         pl.semaphore_signal(barrier, inc=1, device_id={"win": lax.rem(win + step, wins)}, device_id_type=MESH)
-    pl.semaphore_wait(barrier, fibres + wins - 2)
-
-    to_right = pltpu.make_async_remote_copy(
-        src_ref=strain_ref.at[pl.ds(channels - halo, halo)], dst_ref=x_v.at[pl.ds(channels, halo)],
-        send_sem=halo_send.at[0], recv_sem=halo_recv.at[0],
-        device_id={"fibre": lax.rem(me + 1, fibres)}, device_id_type=MESH,
-    )
-    to_left = pltpu.make_async_remote_copy(
-        src_ref=strain_ref.at[pl.ds(0, halo)], dst_ref=x_v.at[pl.ds(channels + halo, halo)],
-        send_sem=halo_send.at[1], recv_sem=halo_recv.at[1],
-        device_id={"fibre": lax.rem(me + fibres - 1, fibres)}, device_id_type=MESH,
-    )
-    first, last = me == 0, me == fibres - 1
-
-    @pl.when(jnp.logical_not(last))
-    def _():
-        to_right.start()
-
-    @pl.when(jnp.logical_not(first))
-    def _():
-        to_left.start()
-
-    @pl.when(first)
-    def _():
-        x_v[channels : channels + halo, :] = jnp.zeros((halo, x_v.shape[1]), x_v.dtype)
-
-    @pl.when(last)
-    def _():
-        x_v[channels + halo :, :] = jnp.zeros((halo, x_v.shape[1]), x_v.dtype)
 
     for low, size, start in ((0, channels, 0), (channels, halo, -halo), (channels + halo, halo, channels)):
         for piece in range(0, size, 64):
@@ -130,6 +103,36 @@
                     jnp.bfloat16
                 )
 
+    pl.semaphore_wait(barrier, fibres + wins - 2)
+
+    to_right = pltpu.make_async_remote_copy(
+        src_ref=strain_ref.at[pl.ds(channels - halo, halo)], dst_ref=x_v.at[pl.ds(channels, halo)],
+        send_sem=halo_send.at[0], recv_sem=halo_recv.at[0],
+        device_id={"fibre": lax.rem(me + 1, fibres)}, device_id_type=MESH,
+    )
+    to_left = pltpu.make_async_remote_copy(
+        src_ref=strain_ref.at[pl.ds(0, halo)], dst_ref=x_v.at[pl.ds(channels + halo, halo)],
+        send_sem=halo_send.at[1], recv_sem=halo_recv.at[1],
+        device_id={"fibre": lax.rem(me + fibres - 1, fibres)}, device_id_type=MESH,
+    )
+    first, last = me == 0, me == fibres - 1
+
+    @pl.when(jnp.logical_not(last))
+    def _():
+        to_right.start()
+
+    @pl.when(jnp.logical_not(first))
+    def _():
+        to_left.start()
+
+    @pl.when(first)
+    def _():
+        x_v[channels : channels + halo, :] = jnp.zeros((halo, x_v.shape[1]), x_v.dtype)
+
+    @pl.when(last)
+    def _():
+        x_v[channels + halo :, :] = jnp.zeros((halo, x_v.shape[1]), x_v.dtype)
+
     load_own.wait()
 
     @pl.when(jnp.logical_not(last))
@@ -143,6 +146,7 @@
         to_right.wait_recv()
 
     load_table.wait()
+    load_phase.wait()
     d_v[...] = lax.dot_general(
         table_v[...], x_v[...], (((1,), (1,)), ((), ())), preferred_element_type=jnp.float32
     )
@@ -165,18 +169,15 @@
         high = both.astype(jnp.bfloat16)
         low = (both - high.astype(jnp.float32)).astype(jnp.bfloat16)
 
-        def banded(place, width):
-            band = band_v[:, place * channels : (place + width) * channels]
-            return jnp.dot(high, band, preferred_element_type=jnp.float32) + jnp.dot(
-                low, band, preferred_element_type=jnp.float32
-            )
-
-        plain = banded(0, 1)
-        real = plain[:bins] - after[0]
-        imag = plain[bins:]
+        parts = jnp.dot(
+            jnp.concatenate([high, low]), band_v[...], preferred_element_type=jnp.float32
+        )
+        shifted = parts[: 2 * bins] + parts[2 * bins :]
+        real = shifted[:bins, :channels] - after[0]
+        imag = shifted[bins:, :channels]
         bin_rows = pl.ds(pl.multiple_of(group * bins, bins), bins)
         for offset in range(1, half_time + 1):
-            pair = banded(2 * offset - 1, 2)
+            pair = shifted[:, (2 * offset - 1) * channels : (2 * offset + 1) * channels]
             ahead_re = pair[:bins, :channels] - before[offset]
             back_re = pair[:bins, channels:]
             if offset in after:
@@ -276,11 +277,13 @@
         right_v[:, :channels] = jnp.stack([real, imag], axis=1).reshape(depth, channels)
         right_v[:, channels:] = jnp.stack([imag, -real], axis=1).reshape(depth, channels)
 
-    row = lax.rem(lax.broadcasted_iota(jnp.int32, (depth, 2 * channels), 0), ROWS)
+    row = lax.broadcasted_iota(jnp.int32, (ROWS, 2 * channels), 0)
+    right = right_v[...].reshape(wins * 2, ROWS, 2 * channels)
+    left = left_v[...]
     for place in range(per_step):
-        here = row == lax.rem(first_bin + place, ROWS)
-        right = jnp.where(here, right_v[...].astype(jnp.float32), 0.0).astype(jnp.bfloat16)
-        result = jnp.dot(left_v[...], right, preferred_element_type=jnp.float32)
+        here = jnp.where(row == lax.rem(first_bin + place, ROWS), 1.0, 0.0).astype(jnp.bfloat16)
+        one_bin = (right * here[None]).reshape(depth, 2 * channels)
+        result = jnp.dot(left, one_bin, preferred_element_type=jnp.float32)
         if not exact:
             result = result * scale
         result = result.astype(jnp.bfloat16)
@@ -304,18 +307,19 @@
         out_shape=jax.ShapeDtypeStruct((fibres, wins, 2, bins, channels), jnp.bfloat16),
         in_specs=[
             pl.BlockSpec(memory_space=pltpu.SMEM),
-            pl.BlockSpec(memory_space=pltpu.VMEM),
-            any_space,
-            any_space,
+            pl.BlockSpec(memory_space=pltpu.HBM),
+            pl.BlockSpec(memory_space=pltpu.HBM),
+            pl.BlockSpec(memory_space=pltpu.HBM),
         ],
         out_specs=any_space,
         scratch_shapes=[
+            pltpu.VMEM(phases.shape, jnp.float32),
             pltpu.VMEM(table.shape, jnp.bfloat16),
             pltpu.VMEM((channels + 2 * halo, samples), jnp.bfloat16),
             pltpu.VMEM((table.shape[0], channels + 2 * halo), jnp.float32),
             pltpu.VMEM((channels + 2 * halo, kernel.shape[1] * channels), jnp.bfloat16),
             pltpu.VMEM((wins, 2, bins, channels), jnp.bfloat16),
-            pltpu.SemaphoreType.DMA((2,)),
+            pltpu.SemaphoreType.DMA((3,)),
             pltpu.SemaphoreType.DMA((2,)),
             pltpu.SemaphoreType.DMA((2,)),
             pltpu.SemaphoreType.DMA((wins,)),
@@ -325,17 +329,18 @@
             pltpu.SemaphoreType.DMA((fibres, wins)),
         ],
         compiler_params=pltpu.CompilerParams(
-            collective_id=0, has_side_effects=True, vmem_limit_bytes=40 * 1024 * 1024
+            collective_id=0, has_side_effects=True, vmem_limit_bytes=60 * 1024 * 1024
         ),
         name="spectra",
     )(kernel.astype(jnp.float32), jnp.asarray(phases), jnp.asarray(table), strain.reshape(channels, samples))
 
     steps = plan.shape[0]
-    chosen = jnp.concatenate([plan, lax.axis_index("fibre").astype(plan.dtype)[None]])
-    per_step = 4
+    per_step = 8
     block = (1, wins, 2, bins, channels)
 
     def pick(place):
+        if place == steps:
+            return pl.BlockSpec(block, lambda i, chosen_ref: (lax.axis_index("fibre"), 0, 0, 0, 0))
         return pl.BlockSpec(block, lambda i, chosen_ref: (chosen_ref[place], 0, 0, 0, 0))
 
     return pl.pallas_call(
@@ -351,9 +356,9 @@
                 pltpu.VMEM((wins * 2 * ROWS, 2 * channels), jnp.bfloat16),
             ],
         ),
-        compiler_params=pltpu.CompilerParams(vmem_limit_bytes=40 * 1024 * 1024),
+        compiler_params=pltpu.CompilerParams(vmem_limit_bytes=60 * 1024 * 1024),
         name="stacks",
-    )(chosen, *([gathered] * (steps + 1)))
+    )(plan, *([gathered] * (steps + 1)))
 
 
 def solution(mesh):

time: 49.5 us -> 45.4 us (0.917)
  local copies, waits for them, and re-layouts: 4.93 us -> 1.38 us
  other arithmetic: 0.73 us -> 0 us
    unnamed x6 -> x0, local copies, waits for them, and re-layouts: 4.15 us -> none
    pallas_call x1, Pallas kernels: 30.9 us -> 32.6 us  [shards(): pl.pallas_call(functools.partial(spectra_kernel, fibres, wins, margin, ha...]
    pallas_call x1, Pallas kernels: 12.7 us -> 11.2 us  [shards(): pl.pallas_call(functools.partial(stack_kernel, steps, 1.0 / math.sqrt(win...]
    concatenate x1 -> x0, other arithmetic: 0.73 us -> none  [shards(): jnp.concatenate([plan, lax.axis_index('fibre').astype(plan.dtype)[None]])]
    convert_element_type x1, local copies, waits for them, and re-layouts: 0.78 us -> 1.38 us  [shards(): kernel.astype(jnp.float32)]
where the time goes in v2:
time: 45.4 us; the launch traced here: 45.2 us
  Pallas kernels  43.8 us (96%)
  local copies, waits for them, and re-layouts  1.38 us (3%)
    pallas_call x1, Pallas kernels, shards(): pl.pallas_call(functools.partial(spectra_kernel, fibres, wins, margin, ha...  32.6 us
    pallas_call x1, Pallas kernels, shards(): pl.pallas_call(functools.partial(stack_kernel, steps, 1.0 / math.sqrt(win...  11.2 us
    convert_element_type x1, local copies, waits for them, and re-layouts, shards(): kernel.astype(jnp.float32)  1.38 us

profile of v2, /device:TPU:0, one launch (start us, length us, event | category | flops | bytes accessed | tf_op | source)
XLA Modules:
  0.0 45.2 jit_solution(15846403153130585014)
XLA Ops:
  0.0 1.4 %copy.7.taps_ref = f32[31,9]{1,0:T(8,128)} copy(bf16[31,9]{0,1:T(8,128)(2,1)} %param.6) | data formatting | bytes 1674 | tf_op jit(solution)/shard_map/convert_element_type | solution.py:335
  1.4 32.6 %spectra.1.refs_0_.refs_1_.refs_2_.refs_3_.refs_4_ = bf16[8,4,2,64,128]{4,3,2,1,0:T(8,128)(2,1)} custom-call(f32[31,9]{1,0:T(8,128)} %copy.7.taps_ref, f32[256,8]{1,0:T(8,128)} %constant.4.clone.phase_hbm, bf16[1040,2048]{1,0:T(8,128)(2,1)} %constant.5.clone.table_ref, bf16[128,2048]{1,0:T(8,128)(2,1)} %bitcast.1), custom_call_target="tpu_custom_call" | custom-call | tf_op jit(solution)/shard_map/spectra/pallas_call | solution.py:305
  34.0 11.2 %stacks.1 = bf16[4,64,2,128,128]{4,3,2,1,0:T(8,128)(2,1)} custom-call(s32[4]{0:T(128)} %chosen_ref.1, bf16[8,4,2,64,128]{4,3,2,1,0:T(8,128)(2,1)} %spectra.1.refs_0_.refs_1_.refs_2_.refs_3_.refs_4_, bf16[8,4,2,64,128]{4,3,2,1,0:T(8,128)(2,1)} %spectra.1.refs_0_.refs_1_.refs_2_.refs_3_.refs_4_, ...), custom_call_target="tpu_custom_call" | custom-call | tf_op jit(solution)/shard_map/stacks/pallas_call | solution.py:346

commit v3 on v2

--- a/solution.py
+++ b/solution.py
@@ -27,6 +27,10 @@
 @functools.lru_cache(maxsize=None)
 def transform_table(samples, bins, half_time):
     index = np.arange(samples, dtype=np.int64)
+    picks = np.zeros((-(-2 * half_time // ROWS) * ROWS, samples), ml_dtypes.bfloat16)
+    for row in range(half_time):
+        picks[row, row] = 1
+        picks[half_time + row, samples - half_time + row] = 1
     blocks = []
     for start in range(0, FB, bins):
         wanted = FLO + start + np.arange(bins, dtype=np.int64)
@@ -34,12 +38,8 @@
         exact = np.concatenate([np.cos(angles), -np.sin(angles)])
         high = exact.astype(ml_dtypes.bfloat16)
         low = (exact - high.astype(np.float64)).astype(ml_dtypes.bfloat16)
-        blocks += [high, low]
-    picks = np.zeros((-(-2 * half_time // ROWS) * ROWS, samples), ml_dtypes.bfloat16)
-    for row in range(half_time):
-        picks[row, row] = 1
-        picks[half_time + row, samples - half_time + row] = 1
-    return np.concatenate(blocks + [picks])
+        blocks += [high, low, picks]
+    return np.concatenate(blocks)
 
 
 @functools.lru_cache(maxsize=None)
@@ -57,7 +57,7 @@
 def spectra_kernel(
     fibres, wins, margin, half_time,
     taps_ref, phase_hbm, table_ref, strain_ref, out_ref,
-    phase_ref, table_v, x_v, d_v, band_v, white_v,
+    phase_ref, table_v, x_v, band_v, white_v,
     load_sem, halo_send, halo_recv, swap_send, swap_recv, keep_sem, gather_send, gather_recv,
 ):
     me = lax.axis_index("fibre")
@@ -81,27 +81,27 @@
     for step in range(1, wins):
         pl.semaphore_signal(barrier, inc=1, device_id={"win": lax.rem(win + step, wins)}, device_id_type=MESH)
 
-    for low, size, start in ((0, channels, 0), (channels, halo, -halo), (channels + halo, halo, channels)):
-        for piece in range(0, size, 64):
-            rows = min(64, size - piece)
-            shape = (rows, channels)
-            lag = (
-                lax.broadcasted_iota(jnp.int32, shape, 0) + (start + piece + margin)
-                - lax.broadcasted_iota(jnp.int32, shape, 1)
-            )
-            totals = [jnp.zeros(shape, jnp.float32)] * len(order)
-            least = start + piece + margin - (channels - 1)
-            most = start + piece + margin + rows - 1
-            for tap in range(max(0, least), min(chan_taps - 1, most) + 1):
-                here = lag == tap
-                totals = [
-                    jnp.where(here, taps_ref[tap, offset + half_time], total)
-                    for total, offset in zip(totals, order)
-                ]
-            for place, total in enumerate(totals):
-                band_v[low + piece : low + piece + rows, place * channels : (place + 1) * channels] = total.astype(
-                    jnp.bfloat16
-                )
+    own_pieces, halo_pieces = channels // ROWS, halo // ROWS
+    slope = lax.broadcasted_iota(jnp.int32, (ROWS, channels), 0) - lax.broadcasted_iota(jnp.int32, (ROWS, channels), 1)
+
+    def band_piece(piece, carry):
+        start = jnp.where(
+            piece < own_pieces, piece * ROWS,
+            jnp.where(piece < own_pieces + halo_pieces, (piece - own_pieces) * ROWS - halo, (piece - halo_pieces) * ROWS),
+        )
+        lag = slope + (start + margin)
+        totals = [jnp.zeros((ROWS, channels), jnp.float32)] * len(order)
+        for tap in range(chan_taps):
+            here = lag == tap
+            totals = [
+                jnp.where(here, taps_ref[tap, offset + half_time], total) for total, offset in zip(totals, order)
+            ]
+        rows = pl.ds(pl.multiple_of(piece * ROWS, ROWS), ROWS)
+        for place, total in enumerate(totals):
+            band_v[rows, place * channels : (place + 1) * channels] = total.astype(jnp.bfloat16)
+        return carry
+
+    lax.fori_loop(0, own_pieces + 2 * halo_pieces, band_piece, 0)
 
     pl.semaphore_wait(barrier, fibres + wins - 2)
 
@@ -147,32 +147,32 @@
 
     load_table.wait()
     load_phase.wait()
-    d_v[...] = lax.dot_general(
-        table_v[...], x_v[...], (((1,), (1,)), ((), ())), preferred_element_type=jnp.float32
-    )
-
-    edges = d_v[4 * FB :, :].astype(jnp.bfloat16)
-    tails = jnp.dot(edges, band_v[...], preferred_element_type=jnp.float32)
-
-    def tail(row, offset):
-        place = order.index(offset)
-        return tails[row : row + 1, place * channels : (place + 1) * channels]
-
-    before = {m: sum(tail(u, m + u) for u in range(half_time - m + 1)) for m in range(1, half_time + 1)}
-    after = {
-        m: sum(tail(2 * half_time - v, -(v + m)) for v in range(1, half_time - m + 1)) for m in range(half_time)
-    }
+    group_rows = table_v.shape[0] // wins
 
     def whiten_group(group):
-        base = pl.multiple_of(group * (4 * bins), 4 * bins)
-        both = d_v[pl.ds(base, 2 * bins), :] + d_v[pl.ds(base + 2 * bins, 2 * bins), :]
+        base = pl.multiple_of(group * group_rows, ROWS)
+        spectra = lax.dot_general(
+            table_v[pl.ds(base, group_rows), :], x_v[...], (((1,), (1,)), ((), ())),
+            preferred_element_type=jnp.float32,
+        )
+        both = spectra[: 2 * bins] + spectra[2 * bins : 4 * bins]
         high = both.astype(jnp.bfloat16)
         low = (both - high.astype(jnp.float32)).astype(jnp.bfloat16)
-
+        edges = spectra[4 * bins :].astype(jnp.bfloat16)
         parts = jnp.dot(
-            jnp.concatenate([high, low]), band_v[...], preferred_element_type=jnp.float32
-        )
-        shifted = parts[: 2 * bins] + parts[2 * bins :]
+            jnp.concatenate([high, low, edges]), band_v[...], preferred_element_type=jnp.float32
+        )
+        tails = parts[4 * bins :]
+
+        def tail(row, offset):
+            place = order.index(offset)
+            return tails[row : row + 1, place * channels : (place + 1) * channels]
+
+        before = {m: sum(tail(u, m + u) for u in range(half_time - m + 1)) for m in range(1, half_time + 1)}
+        after = {
+            m: sum(tail(2 * half_time - v, -(v + m)) for v in range(1, half_time - m + 1)) for m in range(half_time)
+        }
+        shifted = parts[: 2 * bins] + parts[2 * bins : 4 * bins]
         real = shifted[:bins, :channels] - after[0]
         imag = shifted[bins:, :channels]
         bin_rows = pl.ds(pl.multiple_of(group * bins, bins), bins)
@@ -210,11 +210,17 @@
             device_id={"win": source}, device_id_type=MESH,
         )
 
-    steps = sorted(range(1, wins), key=lambda step: -min(step, wins - step))
-    for step in steps:
+    def group_step(turn, carry):
+        step = lax.rem(turn + 1, wins)
         whiten_group(lax.rem(win + step, wins))
-        swap(step).start()
-    whiten_group(win)
+
+        @pl.when(step != 0)
+        def _():
+            swap(step).start()
+
+        return carry
+
+    lax.fori_loop(0, wins, group_step, 0)
     keep = pltpu.make_async_copy(white_v.at[win], out_ref.at[me, win], keep_sem)
     keep.start()
 
@@ -256,40 +262,68 @@
         copy.wait_send()
 
 
-def stack_kernel(steps, scale, chosen_ref, *refs):
-    sources, receiver, out_ref, left_v, right_v = refs[:steps], refs[steps], refs[steps + 1], refs[steps + 2], refs[steps + 3]
-    wins, _, _, channels = receiver.shape[1:]
+def stack_kernel(steps, scale, per_turn, plan_ref, gathered_ref, out_ref, blocks_v, left_v, right_v, result_v, load_sem, out_sem):
+    wins, _, bins, channels = gathered_ref.shape[1:]
     depth = wins * 2 * ROWS
-    per_step = out_ref.shape[1]
-    first_bin = pl.program_id(0) * per_step
     exact = math.frexp(scale)[0] == 0.5
-
-    @pl.when(first_bin % ROWS == 0)
-    def _():
-        group = pl.ds(pl.multiple_of(first_bin // ROWS * ROWS, ROWS), ROWS)
-        for step, source in enumerate(sources):
-            piece = source[0, :, :, group, :].reshape(depth, channels).astype(jnp.float32)
-            if exact:
-                piece = piece * scale
-            left_v[step * channels : (step + 1) * channels, :] = piece.T.astype(jnp.bfloat16)
-        real = receiver[0, :, 0, group, :]
-        imag = receiver[0, :, 1, group, :]
-        right_v[:, :channels] = jnp.stack([real, imag], axis=1).reshape(depth, channels)
-        right_v[:, channels:] = jnp.stack([imag, -real], axis=1).reshape(depth, channels)
-
+    loads = []
+    for place in range(steps + 1):
+        block = plan_ref[place] if place < steps else lax.axis_index("fibre")
+        loads.append(pltpu.make_async_copy(gathered_ref.at[block], blocks_v.at[place], load_sem.at[place]))
+        loads[-1].start()
+    for load in loads:
+        load.wait()
     row = lax.broadcasted_iota(jnp.int32, (ROWS, 2 * channels), 0)
-    right = right_v[...].reshape(wins * 2, ROWS, 2 * channels)
-    left = left_v[...]
-    for place in range(per_step):
-        here = jnp.where(row == lax.rem(first_bin + place, ROWS), 1.0, 0.0).astype(jnp.bfloat16)
-        one_bin = (right * here[None]).reshape(depth, 2 * channels)
-        result = jnp.dot(left, one_bin, preferred_element_type=jnp.float32)
-        if not exact:
-            result = result * scale
-        result = result.astype(jnp.bfloat16)
+
+    def write(turn, step):
+        slot = lax.rem(turn, 2)
+        return pltpu.make_async_copy(
+            result_v.at[slot, step], out_ref.at[step, pl.ds(turn * per_turn, per_turn)], out_sem.at[slot, step]
+        )
+
+    def stack_turn(turn, carry):
+        slot = lax.rem(turn, 2)
+        first_bin = turn * per_turn
+
+        @pl.when(lax.rem(first_bin, ROWS) == 0)
+        def _():
+            group = pl.ds(pl.multiple_of(first_bin, ROWS), ROWS)
+            for step in range(steps):
+                piece = blocks_v[step, :, :, group, :].reshape(depth, channels).astype(jnp.float32)
+                if exact:
+                    piece = piece * scale
+                left_v[step * channels : (step + 1) * channels, :] = piece.T.astype(jnp.bfloat16)
+            real = blocks_v[steps, :, 0, group, :]
+            imag = blocks_v[steps, :, 1, group, :]
+            right_v[:, :channels] = jnp.stack([real, imag], axis=1).reshape(depth, channels)
+            right_v[:, channels:] = jnp.stack([imag, -real], axis=1).reshape(depth, channels)
+
+        @pl.when(turn >= 2)
+        def _():
+            for step in range(steps):
+                write(turn - 2, step).wait()
+
+        right = right_v[...].reshape(wins * 2, ROWS, 2 * channels)
+        left = left_v[...]
+        for place in range(per_turn):
+            here = jnp.where(row == lax.rem(first_bin + place, ROWS), 1.0, 0.0).astype(jnp.bfloat16)
+            one_bin = (right * here[None]).reshape(depth, 2 * channels)
+            result = jnp.dot(left, one_bin, preferred_element_type=jnp.float32)
+            if not exact:
+                result = result * scale
+            result = result.astype(jnp.bfloat16)
+            for step in range(steps):
+                result_v[slot, step, place, 0] = result[step * channels : (step + 1) * channels, :channels]
+                result_v[slot, step, place, 1] = result[step * channels : (step + 1) * channels, channels:]
         for step in range(steps):
-            out_ref[step, place, 0] = result[step * channels : (step + 1) * channels, :channels]
-            out_ref[step, place, 1] = result[step * channels : (step + 1) * channels, channels:]
+            write(turn, step).start()
+        return carry
+
+    turns = bins // per_turn
+    lax.fori_loop(0, turns, stack_turn, 0)
+    for turn in (turns - 2, turns - 1):
+        for step in range(steps):
+            write(turn, step).wait()
 
 
 def shards(strain, kernel, plan):
@@ -316,7 +350,6 @@
             pltpu.VMEM(phases.shape, jnp.float32),
             pltpu.VMEM(table.shape, jnp.bfloat16),
             pltpu.VMEM((channels + 2 * halo, samples), jnp.bfloat16),
-            pltpu.VMEM((table.shape[0], channels + 2 * halo), jnp.float32),
             pltpu.VMEM((channels + 2 * halo, kernel.shape[1] * channels), jnp.bfloat16),
             pltpu.VMEM((wins, 2, bins, channels), jnp.bfloat16),
             pltpu.SemaphoreType.DMA((3,)),
@@ -335,30 +368,23 @@
     )(kernel.astype(jnp.float32), jnp.asarray(phases), jnp.asarray(table), strain.reshape(channels, samples))
 
     steps = plan.shape[0]
-    per_step = 8
-    block = (1, wins, 2, bins, channels)
-
-    def pick(place):
-        if place == steps:
-            return pl.BlockSpec(block, lambda i, chosen_ref: (lax.axis_index("fibre"), 0, 0, 0, 0))
-        return pl.BlockSpec(block, lambda i, chosen_ref: (chosen_ref[place], 0, 0, 0, 0))
-
+    per_turn = 4
     return pl.pallas_call(
-        functools.partial(stack_kernel, steps, 1.0 / math.sqrt(wins * own_windows)),
+        functools.partial(stack_kernel, steps, 1.0 / math.sqrt(wins * own_windows), per_turn),
         out_shape=jax.ShapeDtypeStruct((steps, bins, 2, channels, channels), jnp.bfloat16),
-        grid_spec=pltpu.PrefetchScalarGridSpec(
-            num_scalar_prefetch=1,
-            grid=(bins // per_step,),
-            in_specs=[pick(place) for place in range(steps + 1)],
-            out_specs=pl.BlockSpec((steps, per_step, 2, channels, channels), lambda i, chosen_ref: (0, i, 0, 0, 0)),
-            scratch_shapes=[
-                pltpu.VMEM((steps * channels, wins * 2 * ROWS), jnp.bfloat16),
-                pltpu.VMEM((wins * 2 * ROWS, 2 * channels), jnp.bfloat16),
-            ],
-        ),
+        in_specs=[pl.BlockSpec(memory_space=pltpu.SMEM), any_space],
+        out_specs=any_space,
+        scratch_shapes=[
+            pltpu.VMEM((steps + 1, wins, 2, bins, channels), jnp.bfloat16),
+            pltpu.VMEM((steps * channels, wins * 2 * ROWS), jnp.bfloat16),
+            pltpu.VMEM((wins * 2 * ROWS, 2 * channels), jnp.bfloat16),
+            pltpu.VMEM((2, steps, per_turn, 2, channels, channels), jnp.bfloat16),
+            pltpu.SemaphoreType.DMA((steps + 1,)),
+            pltpu.SemaphoreType.DMA((2, steps)),
+        ],
         compiler_params=pltpu.CompilerParams(vmem_limit_bytes=60 * 1024 * 1024),
         name="stacks",
-    )(plan, *([gathered] * (steps + 1)))
+    )(plan, gathered)
 
 
 def solution(mesh):

time: 45.4 us -> 48.3 us (1.064)
  Pallas kernels: 43.8 us -> 46.7 us
    pallas_call x1, Pallas kernels: 11.2 us -> 13.5 us  [shards(): pl.pallas_call(functools.partial(stack_kernel, steps, 1.0 / math.sqrt(win...]
    pallas_call x1, Pallas kernels: 32.6 us -> 33.2 us  [shards(): pl.pallas_call(functools.partial(spectra_kernel, fibres, wins, margin, ha...]
where the time goes in v3:
time: 48.3 us; the launch traced here: 48.1 us
  Pallas kernels  46.7 us (97%)
  local copies, waits for them, and re-layouts  1.38 us (3%)
    pallas_call x1, Pallas kernels, shards(): pl.pallas_call(functools.partial(spectra_kernel, fibres, wins, margin, ha...  33.2 us
    pallas_call x1, Pallas kernels, shards(): pl.pallas_call(functools.partial(stack_kernel, steps, 1.0 / math.sqrt(win...  13.5 us
    convert_element_type x1, local copies, waits for them, and re-layouts, shards(): kernel.astype(jnp.float32)  1.38 us

profile of v3, /device:TPU:0, one launch (start us, length us, event | category | flops | bytes accessed | tf_op | source)
XLA Modules:
  0.0 48.1 jit_solution(3416729590674706259)
XLA Ops:
  0.0 1.4 %copy.7.taps_ref = f32[31,9]{1,0:T(8,128)} copy(bf16[31,9]{0,1:T(8,128)(2,1)} %param.6) | data formatting | bytes 1674 | tf_op jit(solution)/shard_map/convert_element_type | solution.py:368
  1.4 33.2 %spectra.1.gathered_ref = bf16[8,4,2,64,128]{4,3,2,1,0:T(8,128)(2,1)} custom-call(f32[31,9]{1,0:T(8,128)} %copy.7.taps_ref, f32[256,8]{1,0:T(8,128)} %constant.4.clone.phase_hbm, bf16[1088,2048]{1,0:T(8,128)(2,1)} %constant.5.clone.table_ref, bf16[128,2048]{1,0:T(8,128)(2,1)} %bitcast.1), custom_call_target="tpu_custom_call" | custom-call | tf_op jit(solution)/shard_map/spectra/pallas_call | solution.py:339
  34.6 13.5 %stacks.1 = bf16[4,64,2,128,128]{4,3,2,1,0:T(8,128)(2,1)} custom-call(s32[4]{0:T(128)} %plan_ref.1, bf16[8,4,2,64,128]{4,3,2,1,0:T(8,128)(2,1)} %spectra.1.gathered_ref), custom_call_target="tpu_custom_call" | custom-call | tf_op jit(solution)/shard_map/stacks/pallas_call | solution.py:372

commit v4 on v3

--- a/solution.py
+++ b/solution.py
@@ -57,7 +57,7 @@
 def spectra_kernel(
     fibres, wins, margin, half_time,
     taps_ref, phase_hbm, table_ref, strain_ref, out_ref,
-    phase_ref, table_v, x_v, band_v, white_v,
+    phase_ref, table_v, x_v, xt_v, band_v, white_v,
     load_sem, halo_send, halo_recv, swap_send, swap_recv, keep_sem, gather_send, gather_recv,
 ):
     me = lax.axis_index("fibre")
@@ -80,29 +80,6 @@
         pl.semaphore_signal(barrier, inc=1, device_id={"fibre": lax.rem(me + step, fibres)}, device_id_type=MESH)
     for step in range(1, wins):
         pl.semaphore_signal(barrier, inc=1, device_id={"win": lax.rem(win + step, wins)}, device_id_type=MESH)
-
-    own_pieces, halo_pieces = channels // ROWS, halo // ROWS
-    slope = lax.broadcasted_iota(jnp.int32, (ROWS, channels), 0) - lax.broadcasted_iota(jnp.int32, (ROWS, channels), 1)
-
-    def band_piece(piece, carry):
-        start = jnp.where(
-            piece < own_pieces, piece * ROWS,
-            jnp.where(piece < own_pieces + halo_pieces, (piece - own_pieces) * ROWS - halo, (piece - halo_pieces) * ROWS),
-        )
-        lag = slope + (start + margin)
-        totals = [jnp.zeros((ROWS, channels), jnp.float32)] * len(order)
-        for tap in range(chan_taps):
-            here = lag == tap
-            totals = [
-                jnp.where(here, taps_ref[tap, offset + half_time], total) for total, offset in zip(totals, order)
-            ]
-        rows = pl.ds(pl.multiple_of(piece * ROWS, ROWS), ROWS)
-        for place, total in enumerate(totals):
-            band_v[rows, place * channels : (place + 1) * channels] = total.astype(jnp.bfloat16)
-        return carry
-
-    lax.fori_loop(0, own_pieces + 2 * halo_pieces, band_piece, 0)
-
     pl.semaphore_wait(barrier, fibres + wins - 2)
 
     to_right = pltpu.make_async_remote_copy(
@@ -135,6 +112,33 @@
 
     load_own.wait()
 
+    def turn_over(piece, carry):
+        columns = pl.ds(pl.multiple_of(piece * 256, 256), 256)
+        xt_v[columns, :channels] = x_v[:channels, columns].astype(jnp.float32).T.astype(jnp.bfloat16)
+        return carry
+
+    lax.fori_loop(0, x_v.shape[1] // 256, turn_over, 0)
+
+    def band_rows(first_row, rows, source):
+        lag = source - lax.broadcasted_iota(jnp.int32, (rows, channels), 1) + margin
+        totals = [jnp.zeros((rows, channels), jnp.float32)] * len(order)
+        for tap in range(chan_taps):
+            here = lag == tap
+            totals = [
+                jnp.where(here, taps_ref[tap, offset + half_time], total) for total, offset in zip(totals, order)
+            ]
+        for place, total in enumerate(totals):
+            band_v[pl.ds(first_row, rows), place * channels : (place + 1) * channels] = total.astype(jnp.bfloat16)
+
+    def own_rows(piece, carry):
+        first_row = pl.multiple_of(piece * 2 * ROWS, 2 * ROWS)
+        band_rows(first_row, 2 * ROWS, lax.broadcasted_iota(jnp.int32, (2 * ROWS, channels), 0) + first_row)
+        return carry
+
+    lax.fori_loop(0, channels // (2 * ROWS), own_rows, 0)
+    row = lax.broadcasted_iota(jnp.int32, (2 * halo, channels), 0)
+    band_rows(channels, 2 * halo, row - halo + jnp.where(row < halo, 0, channels))
+
     @pl.when(jnp.logical_not(last))
     def _():
         to_right.wait_send()
@@ -145,15 +149,15 @@
         to_left.wait_send()
         to_right.wait_recv()
 
+    xt_v[:, channels:] = x_v[channels:, :].astype(jnp.float32).T.astype(jnp.bfloat16)
     load_table.wait()
     load_phase.wait()
     group_rows = table_v.shape[0] // wins
 
     def whiten_group(group):
         base = pl.multiple_of(group * group_rows, ROWS)
-        spectra = lax.dot_general(
-            table_v[pl.ds(base, group_rows), :], x_v[...], (((1,), (1,)), ((), ())),
-            preferred_element_type=jnp.float32,
+        spectra = jnp.dot(
+            table_v[pl.ds(base, group_rows), :], xt_v[...], preferred_element_type=jnp.float32
         )
         both = spectra[: 2 * bins] + spectra[2 * bins : 4 * bins]
         high = both.astype(jnp.bfloat16)
@@ -305,16 +309,19 @@
 
         right = right_v[...].reshape(wins * 2, ROWS, 2 * channels)
         left = left_v[...]
-        for place in range(per_turn):
-            here = jnp.where(row == lax.rem(first_bin + place, ROWS), 1.0, 0.0).astype(jnp.bfloat16)
-            one_bin = (right * here[None]).reshape(depth, 2 * channels)
-            result = jnp.dot(left, one_bin, preferred_element_type=jnp.float32)
+        for pair in range(0, per_turn, 2):
+            columns = []
+            for place in (pair, pair + 1):
+                here = jnp.where(row == lax.rem(first_bin + place, ROWS), 1.0, 0.0).astype(jnp.bfloat16)
+                columns.append((right * here[None]).reshape(depth, 2 * channels))
+            result = jnp.dot(left, jnp.concatenate(columns, axis=1), preferred_element_type=jnp.float32)
             if not exact:
                 result = result * scale
             result = result.astype(jnp.bfloat16)
             for step in range(steps):
-                result_v[slot, step, place, 0] = result[step * channels : (step + 1) * channels, :channels]
-                result_v[slot, step, place, 1] = result[step * channels : (step + 1) * channels, channels:]
+                rows = result[step * channels : (step + 1) * channels]
+                for part in range(4):
+                    result_v[slot, step, pair + part // 2, part % 2] = rows[:, part * channels : (part + 1) * channels]
         for step in range(steps):
             write(turn, step).start()
         return carry
@@ -350,6 +357,7 @@
             pltpu.VMEM(phases.shape, jnp.float32),
             pltpu.VMEM(table.shape, jnp.bfloat16),
             pltpu.VMEM((channels + 2 * halo, samples), jnp.bfloat16),
+            pltpu.VMEM((samples, channels + 2 * halo), jnp.bfloat16),
             pltpu.VMEM((channels + 2 * halo, kernel.shape[1] * channels), jnp.bfloat16),
             pltpu.VMEM((wins, 2, bins, channels), jnp.bfloat16),
             pltpu.SemaphoreType.DMA((3,)),
@@ -368,7 +376,7 @@
     )(kernel.astype(jnp.float32), jnp.asarray(phases), jnp.asarray(table), strain.reshape(channels, samples))
 
     steps = plan.shape[0]
-    per_turn = 4
+    per_turn = 8
     return pl.pallas_call(
         functools.partial(stack_kernel, steps, 1.0 / math.sqrt(wins * own_windows), per_turn),
         out_shape=jax.ShapeDtypeStruct((steps, bins, 2, channels, channels), jnp.bfloat16),

time: 48.3 us -> 45.5 us (0.942)
  Pallas kernels: 46.7 us -> 43.9 us
    pallas_call x1, Pallas kernels: 13.5 us -> 10.7 us  [shards(): pl.pallas_call(functools.partial(stack_kernel, steps, 1.0 / math.sqrt(win...]
where the time goes in v4:
time: 45.5 us; the launch traced here: 45.3 us
  Pallas kernels  43.9 us (96%)
  local copies, waits for them, and re-layouts  1.38 us (3%)
    pallas_call x1, Pallas kernels, shards(): pl.pallas_call(functools.partial(spectra_kernel, fibres, wins, margin, ha...  33.2 us
    pallas_call x1, Pallas kernels, shards(): pl.pallas_call(functools.partial(stack_kernel, steps, 1.0 / math.sqrt(win...  10.7 us
    convert_element_type x1, local copies, waits for them, and re-layouts, shards(): kernel.astype(jnp.float32)  1.38 us

profile of v4, /device:TPU:0, one launch (start us, length us, event | category | flops | bytes accessed | tf_op | source)
XLA Modules:
  0.0 45.3 jit_solution(15587814020491855559)
XLA Ops:
  0.0 1.4 %copy.7.taps_ref = f32[31,9]{1,0:T(8,128)} copy(bf16[31,9]{0,1:T(8,128)(2,1)} %param.6) | data formatting | bytes 1674 | tf_op jit(solution)/shard_map/convert_element_type | solution.py:376
  1.4 33.2 %spectra.1.gathered_ref = bf16[8,4,2,64,128]{4,3,2,1,0:T(8,128)(2,1)} custom-call(f32[31,9]{1,0:T(8,128)} %copy.7.taps_ref, f32[256,8]{1,0:T(8,128)} %constant.4.clone.phase_hbm, bf16[1088,2048]{1,0:T(8,128)(2,1)} %constant.5.clone.table_ref, bf16[128,2048]{1,0:T(8,128)(2,1)} %bitcast.1), custom_call_target="tpu_custom_call" | custom-call | tf_op jit(solution)/shard_map/spectra/pallas_call | solution.py:346
  34.6 10.7 %stacks.1 = bf16[4,64,2,128,128]{4,3,2,1,0:T(8,128)(2,1)} custom-call(s32[4]{0:T(128)} %plan_ref.1, bf16[8,4,2,64,128]{4,3,2,1,0:T(8,128)(2,1)} %spectra.1.gathered_ref), custom_call_target="tpu_custom_call" | custom-call | tf_op jit(solution)/shard_map/stacks/pallas_call | solution.py:380

commit v5 on v4

--- a/solution.py
+++ b/solution.py
@@ -57,7 +57,7 @@
 def spectra_kernel(
     fibres, wins, margin, half_time,
     taps_ref, phase_hbm, table_ref, strain_ref, out_ref,
-    phase_ref, table_v, x_v, xt_v, band_v, white_v,
+    phase_ref, table_v, x_v, xt_v, band_v, white_v, held_v,
     load_sem, halo_send, halo_recv, swap_send, swap_recv, keep_sem, gather_send, gather_recv,
 ):
     me = lax.axis_index("fibre")
@@ -154,7 +154,7 @@
     load_phase.wait()
     group_rows = table_v.shape[0] // wins
 
-    def whiten_group(group):
+    def whiten_group(group, into):
         base = pl.multiple_of(group * group_rows, ROWS)
         spectra = jnp.dot(
             table_v[pl.ds(base, group_rows), :], xt_v[...], preferred_element_type=jnp.float32
@@ -195,13 +195,13 @@
         for start in range(0, bins, BLK):
             level = jnp.mean(magnitude[start : start + BLK], axis=0, keepdims=True) + 1e-06
             factor = 1.0 / level
-            white_v[group, 0, start : start + BLK] = (real[start : start + BLK] * factor).astype(jnp.bfloat16)
-            white_v[group, 1, start : start + BLK] = (imag[start : start + BLK] * factor).astype(jnp.bfloat16)
+            into[0, start : start + BLK] = (real[start : start + BLK] * factor).astype(jnp.bfloat16)
+            into[1, start : start + BLK] = (imag[start : start + BLK] * factor).astype(jnp.bfloat16)
 
     def swap(step):
         target = lax.rem(win + step, wins)
         return pltpu.make_async_remote_copy(
-            src_ref=white_v.at[target], dst_ref=out_ref.at[me, win],
+            src_ref=white_v.at[target], dst_ref=held_v.at[me, win],
             send_sem=swap_send.at[step], recv_sem=swap_recv.at[step],
             device_id={"win": target}, device_id_type=MESH,
         )
@@ -209,48 +209,27 @@
     def swap_arrival(step):
         source = lax.rem(win + wins - step, wins)
         return pltpu.make_async_remote_copy(
-            src_ref=white_v.at[win], dst_ref=out_ref.at[me, source],
+            src_ref=white_v.at[win], dst_ref=held_v.at[me, source],
             send_sem=swap_send.at[step], recv_sem=swap_recv.at[step],
             device_id={"win": source}, device_id_type=MESH,
         )
 
-    def group_step(turn, carry):
-        step = lax.rem(turn + 1, wins)
-        whiten_group(lax.rem(win + step, wins))
-
-        @pl.when(step != 0)
-        def _():
-            swap(step).start()
-
-        return carry
-
-    lax.fori_loop(0, wins, group_step, 0)
-    keep = pltpu.make_async_copy(white_v.at[win], out_ref.at[me, win], keep_sem)
-    keep.start()
-
     orders = gather_orders(fibres)
-    arrival_order = [0] + sorted(range(1, wins), key=lambda step: min(step, wins - step))
 
     def hop(step, away, bit):
         block = lax.bitwise_xor(me, away)
         window = lax.rem(win + wins - step, wins)
-        source = white_v.at[win] if step == 0 and away == 0 else out_ref.at[block, window]
         return pltpu.make_async_remote_copy(
-            src_ref=source, dst_ref=out_ref.at[block, window],
+            src_ref=held_v.at[block, window], dst_ref=held_v.at[block, window],
             send_sem=gather_send.at[away ^ bit, step], recv_sem=gather_recv.at[away ^ bit, step],
             device_id={"fibre": lax.bitwise_xor(me, bit)}, device_id_type=MESH,
         )
 
-    events = []
-    for rank, step in enumerate(arrival_order):
-        line = orders[rank % 2]
-        for away in range(fibres):
-            taken = [place for place, bit in enumerate(line) if away & bit]
-            latest = max(taken, default=-1)
-            events.append((rank + len(taken), rank, latest, away, step, line))
-    events.sort(key=lambda event: event[:4])
     started = []
-    for _, _, latest, away, step, line in events:
+
+    def settle(step, away):
+        line = orders[step % 2]
+        latest = max([place for place, bit in enumerate(line) if away & bit], default=-1)
         if away:
             hop(step, away ^ line[latest], line[latest]).wait_recv()
         elif step:
@@ -259,14 +238,34 @@
             copy = hop(step, away, bit)
             copy.start()
             started.append(copy)
-    keep.wait()
+        block, window = lax.bitwise_xor(me, away), lax.rem(win + wins - step, wins)
+        pltpu.make_async_copy(held_v.at[block, window], out_ref.at[block, window], keep_sem).start()
+
+    events = sorted(
+        (step + away.bit_count(), step, [away & bit != 0 for bit in orders[step % 2]][::-1], away)
+        for step in range(wins) for away in range(fibres)
+    )
+    for turn in range(wins):
+        if turn:
+            target = lax.rem(win + turn, wins)
+            whiten_group(target, white_v.at[target])
+            swap(turn).start()
+        else:
+            whiten_group(win, held_v.at[me, win])
+        due = [event for event in events if event[0] + (2 if event[1] else 1 if event[3] else 0) <= turn]
+        events = [event for event in events if event not in due]
+        for _, step, _, away in due:
+            settle(step, away)
+    for _, step, _, away in events:
+        settle(step, away)
     for step in range(1, wins):
         swap(step).wait_send()
     for copy in started:
         copy.wait_send()
-
-
-def stack_kernel(steps, scale, per_turn, plan_ref, gathered_ref, out_ref, blocks_v, left_v, right_v, result_v, load_sem, out_sem):
+    pltpu.make_async_copy(held_v, out_ref, keep_sem).wait()
+
+
+def stack_kernel(steps, scale, plan_ref, gathered_ref, out_ref, blocks_v, left_v, right_v, result_v, load_sem, out_sem):
     wins, _, bins, channels = gathered_ref.shape[1:]
     depth = wins * 2 * ROWS
     exact = math.frexp(scale)[0] == 0.5
@@ -279,58 +278,50 @@
         load.wait()
     row = lax.broadcasted_iota(jnp.int32, (ROWS, 2 * channels), 0)
 
-    def write(turn, step):
-        slot = lax.rem(turn, 2)
-        return pltpu.make_async_copy(
-            result_v.at[slot, step], out_ref.at[step, pl.ds(turn * per_turn, per_turn)], out_sem.at[slot, step]
-        )
-
-    def stack_turn(turn, carry):
-        slot = lax.rem(turn, 2)
-        first_bin = turn * per_turn
-
-        @pl.when(lax.rem(first_bin, ROWS) == 0)
-        def _():
-            group = pl.ds(pl.multiple_of(first_bin, ROWS), ROWS)
-            for step in range(steps):
-                piece = blocks_v[step, :, :, group, :].reshape(depth, channels).astype(jnp.float32)
-                if exact:
-                    piece = piece * scale
-                left_v[step * channels : (step + 1) * channels, :] = piece.T.astype(jnp.bfloat16)
-            real = blocks_v[steps, :, 0, group, :]
-            imag = blocks_v[steps, :, 1, group, :]
-            right_v[:, :channels] = jnp.stack([real, imag], axis=1).reshape(depth, channels)
-            right_v[:, channels:] = jnp.stack([imag, -real], axis=1).reshape(depth, channels)
-
-        @pl.when(turn >= 2)
-        def _():
-            for step in range(steps):
-                write(turn - 2, step).wait()
-
+    pairs = ROWS // 2
+
+    def write(group, pair):
+        bin_pair = pl.ds(group * ROWS + 2 * pair, 2)
+        return pltpu.make_async_copy(result_v.at[pair], out_ref.at[:, bin_pair], out_sem.at[pair])
+
+    def stack_group(group, carry):
+        rows = pl.ds(pl.multiple_of(group * ROWS, ROWS), ROWS)
+        for step in range(steps):
+            piece = blocks_v[step, :, :, rows, :].reshape(depth, channels).astype(jnp.float32)
+            if exact:
+                piece = piece * scale
+            left_v[step * channels : (step + 1) * channels, :] = piece.T.astype(jnp.bfloat16)
+        real = blocks_v[steps, :, 0, rows, :]
+        imag = blocks_v[steps, :, 1, rows, :]
+        right_v[:, :channels] = jnp.stack([real, imag], axis=1).reshape(depth, channels)
+        right_v[:, channels:] = jnp.stack([imag, -real], axis=1).reshape(depth, channels)
         right = right_v[...].reshape(wins * 2, ROWS, 2 * channels)
         left = left_v[...]
-        for pair in range(0, per_turn, 2):
+        for pair in range(pairs):
             columns = []
-            for place in (pair, pair + 1):
-                here = jnp.where(row == lax.rem(first_bin + place, ROWS), 1.0, 0.0).astype(jnp.bfloat16)
+            for place in (2 * pair, 2 * pair + 1):
+                here = jnp.where(row == place, 1.0, 0.0).astype(jnp.bfloat16)
                 columns.append((right * here[None]).reshape(depth, 2 * channels))
             result = jnp.dot(left, jnp.concatenate(columns, axis=1), preferred_element_type=jnp.float32)
             if not exact:
                 result = result * scale
             result = result.astype(jnp.bfloat16)
+
+            @pl.when(group > 0)
+            def _():
+                write(group - 1, pair).wait()
+
             for step in range(steps):
-                rows = result[step * channels : (step + 1) * channels]
+                one_step = result[step * channels : (step + 1) * channels]
                 for part in range(4):
-                    result_v[slot, step, pair + part // 2, part % 2] = rows[:, part * channels : (part + 1) * channels]
-        for step in range(steps):
-            write(turn, step).start()
+                    result_v[pair, step, part // 2, part % 2] = one_step[:, part * channels : (part + 1) * channels]
+            write(group, pair).start()
         return carry
 
-    turns = bins // per_turn
-    lax.fori_loop(0, turns, stack_turn, 0)
-    for turn in (turns - 2, turns - 1):
-        for step in range(steps):
-            write(turn, step).wait()
+    groups = bins // ROWS
+    lax.fori_loop(0, groups, stack_group, 0)
+    for pair in range(pairs):
+        write(groups - 1, pair).wait()
 
 
 def shards(strain, kernel, plan):
@@ -360,6 +351,7 @@
             pltpu.VMEM((samples, channels + 2 * halo), jnp.bfloat16),
             pltpu.VMEM((channels + 2 * halo, kernel.shape[1] * channels), jnp.bfloat16),
             pltpu.VMEM((wins, 2, bins, channels), jnp.bfloat16),
+            pltpu.VMEM((fibres, wins, 2, bins, channels), jnp.bfloat16),
             pltpu.SemaphoreType.DMA((3,)),
             pltpu.SemaphoreType.DMA((2,)),
             pltpu.SemaphoreType.DMA((2,)),
@@ -376,9 +368,8 @@
     )(kernel.astype(jnp.float32), jnp.asarray(phases), jnp.asarray(table), strain.reshape(channels, samples))
 
     steps = plan.shape[0]
-    per_turn = 8
     return pl.pallas_call(
-        functools.partial(stack_kernel, steps, 1.0 / math.sqrt(wins * own_windows), per_turn),
+        functools.partial(stack_kernel, steps, 1.0 / math.sqrt(wins * own_windows)),
         out_shape=jax.ShapeDtypeStruct((steps, bins, 2, channels, channels), jnp.bfloat16),
         in_specs=[pl.BlockSpec(memory_space=pltpu.SMEM), any_space],
         out_specs=any_space,
@@ -386,9 +377,9 @@
             pltpu.VMEM((steps + 1, wins, 2, bins, channels), jnp.bfloat16),
             pltpu.VMEM((steps * channels, wins * 2 * ROWS), jnp.bfloat16),
             pltpu.VMEM((wins * 2 * ROWS, 2 * channels), jnp.bfloat16),
-            pltpu.VMEM((2, steps, per_turn, 2, channels, channels), jnp.bfloat16),
+            pltpu.VMEM((ROWS // 2, steps, 2, 2, channels, channels), jnp.bfloat16),
             pltpu.SemaphoreType.DMA((steps + 1,)),
-            pltpu.SemaphoreType.DMA((2, steps)),
+            pltpu.SemaphoreType.DMA((ROWS // 2,)),
         ],
         compiler_params=pltpu.CompilerParams(vmem_limit_bytes=60 * 1024 * 1024),
         name="stacks",

time: 45.5 us -> 44.9 us (0.987); the launches traced: 45.3 us -> 44.1 us
  Pallas kernels: 43.9 us -> 42.7 us
    pallas_call x1, Pallas kernels: 33.2 us -> 29.9 us  [shards(): pl.pallas_call(functools.partial(spectra_kernel, fibres, wins, margin, ha...]
    pallas_call x1, Pallas kernels: 10.7 us -> 12.8 us  [shards(): pl.pallas_call(functools.partial(stack_kernel, steps, 1.0 / math.sqrt(win...]
where the time goes in v5:
time: 44.9 us; the launch traced here: 44.1 us
  Pallas kernels  42.7 us (95%)
  local copies, waits for them, and re-layouts  1.38 us (3%)
    pallas_call x1, Pallas kernels, shards(): pl.pallas_call(functools.partial(spectra_kernel, fibres, wins, margin, ha...  29.9 us
    pallas_call x1, Pallas kernels, shards(): pl.pallas_call(functools.partial(stack_kernel, steps, 1.0 / math.sqrt(win...  12.8 us
    convert_element_type x1, local copies, waits for them, and re-layouts, shards(): kernel.astype(jnp.float32)  1.38 us

profile of v5, /device:TPU:0, one launch (start us, length us, event | category | flops | bytes accessed | tf_op | source)
XLA Modules:
  0.0 44.1 jit_solution(15082732832840488773)
XLA Ops:
  0.0 1.4 %copy.7.taps_ref = f32[31,9]{1,0:T(8,128)} copy(bf16[31,9]{0,1:T(8,128)(2,1)} %param.6) | data formatting | bytes 1674 | tf_op jit(solution)/shard_map/convert_element_type | solution.py:368
  1.4 29.9 %spectra.1.gathered_ref = bf16[8,4,2,64,128]{4,3,2,1,0:T(8,128)(2,1)} custom-call(f32[31,9]{1,0:T(8,128)} %copy.7.taps_ref, f32[256,8]{1,0:T(8,128)} %constant.4.clone.phase_hbm, bf16[1088,2048]{1,0:T(8,128)(2,1)} %constant.5.clone.table_ref, bf16[128,2048]{1,0:T(8,128)(2,1)} %bitcast.1), custom_call_target="tpu_custom_call" | custom-call | tf_op jit(solution)/shard_map/spectra/pallas_call | solution.py:337
  31.3 12.8 %stacks.1 = bf16[4,64,2,128,128]{4,3,2,1,0:T(8,128)(2,1)} custom-call(s32[4]{0:T(128)} %plan_ref.1, bf16[8,4,2,64,128]{4,3,2,1,0:T(8,128)(2,1)} %spectra.1.gathered_ref), custom_call_target="tpu_custom_call" | custom-call | tf_op jit(solution)/shard_map/stacks/pallas_call | solution.py:371

commit v6 on v4

--- a/solution.py
+++ b/solution.py
@@ -56,8 +56,8 @@
 
 def spectra_kernel(
     fibres, wins, margin, half_time,
-    taps_ref, phase_hbm, table_ref, strain_ref, out_ref,
-    phase_ref, table_v, x_v, xt_v, band_v, white_v,
+    taps_hbm, phase_hbm, table_ref, strain_ref, out_ref,
+    taps_ref, phase_ref, table_v, x_v, xt_v, band_v, white_v, held_v,
     load_sem, halo_send, halo_recv, swap_send, swap_recv, keep_sem, gather_send, gather_recv,
 ):
     me = lax.axis_index("fibre")
@@ -74,6 +74,8 @@
     load_own.start()
     load_phase = pltpu.make_async_copy(phase_hbm, phase_ref, load_sem.at[2])
     load_phase.start()
+    load_taps = pltpu.make_async_copy(taps_hbm, taps_ref, load_sem.at[3])
+    load_taps.start()
 
     barrier = pltpu.get_barrier_semaphore()
     for step in range(1, fibres):
@@ -119,6 +121,8 @@
 
     lax.fori_loop(0, x_v.shape[1] // 256, turn_over, 0)
 
+    load_taps.wait()
+
     def band_rows(first_row, rows, source):
         lag = source - lax.broadcasted_iota(jnp.int32, (rows, channels), 1) + margin
         totals = [jnp.zeros((rows, channels), jnp.float32)] * len(order)
@@ -154,7 +158,7 @@
     load_phase.wait()
     group_rows = table_v.shape[0] // wins
 
-    def whiten_group(group):
+    def whiten_group(group, into):
         base = pl.multiple_of(group * group_rows, ROWS)
         spectra = jnp.dot(
             table_v[pl.ds(base, group_rows), :], xt_v[...], preferred_element_type=jnp.float32
@@ -195,75 +199,92 @@
         for start in range(0, bins, BLK):
             level = jnp.mean(magnitude[start : start + BLK], axis=0, keepdims=True) + 1e-06
             factor = 1.0 / level
-            white_v[group, 0, start : start + BLK] = (real[start : start + BLK] * factor).astype(jnp.bfloat16)
-            white_v[group, 1, start : start + BLK] = (imag[start : start + BLK] * factor).astype(jnp.bfloat16)
+            into[0, start : start + BLK] = (real[start : start + BLK] * factor).astype(jnp.bfloat16)
+            into[1, start : start + BLK] = (imag[start : start + BLK] * factor).astype(jnp.bfloat16)
 
     def swap(step):
-        target = lax.rem(win + step, wins)
+        target = lax.bitwise_xor(win, step)
         return pltpu.make_async_remote_copy(
-            src_ref=white_v.at[target], dst_ref=out_ref.at[me, win],
+            src_ref=white_v.at[target], dst_ref=held_v.at[me, win],
             send_sem=swap_send.at[step], recv_sem=swap_recv.at[step],
             device_id={"win": target}, device_id_type=MESH,
         )
 
     def swap_arrival(step):
-        source = lax.rem(win + wins - step, wins)
+        source = lax.bitwise_xor(win, step)
         return pltpu.make_async_remote_copy(
-            src_ref=white_v.at[win], dst_ref=out_ref.at[me, source],
+            src_ref=white_v.at[win], dst_ref=held_v.at[me, source],
             send_sem=swap_send.at[step], recv_sem=swap_recv.at[step],
             device_id={"win": source}, device_id_type=MESH,
         )
 
-    def group_step(turn, carry):
-        step = lax.rem(turn + 1, wins)
-        whiten_group(lax.rem(win + step, wins))
-
-        @pl.when(step != 0)
-        def _():
-            swap(step).start()
-
-        return carry
-
-    lax.fori_loop(0, wins, group_step, 0)
-    keep = pltpu.make_async_copy(white_v.at[win], out_ref.at[me, win], keep_sem)
-    keep.start()
-
     orders = gather_orders(fibres)
-    arrival_order = [0] + sorted(range(1, wins), key=lambda step: min(step, wins - step))
 
     def hop(step, away, bit):
         block = lax.bitwise_xor(me, away)
-        window = lax.rem(win + wins - step, wins)
-        source = white_v.at[win] if step == 0 and away == 0 else out_ref.at[block, window]
+        window = lax.bitwise_xor(win, step)
         return pltpu.make_async_remote_copy(
-            src_ref=source, dst_ref=out_ref.at[block, window],
+            src_ref=held_v.at[block, window], dst_ref=held_v.at[block, window],
             send_sem=gather_send.at[away ^ bit, step], recv_sem=gather_recv.at[away ^ bit, step],
             device_id={"fibre": lax.bitwise_xor(me, bit)}, device_id_type=MESH,
         )
 
-    events = []
-    for rank, step in enumerate(arrival_order):
-        line = orders[rank % 2]
-        for away in range(fibres):
-            taken = [place for place, bit in enumerate(line) if away & bit]
-            latest = max(taken, default=-1)
-            events.append((rank + len(taken), rank, latest, away, step, line))
-    events.sort(key=lambda event: event[:4])
     started = []
-    for _, _, latest, away, step, line in events:
-        if away:
-            hop(step, away ^ line[latest], line[latest]).wait_recv()
+
+    turns = [0] + list(range(wins - 1, 0, -1))
+
+    def route(step, away):
+        place = turns.index(step)
+        if place < wins // 2:
+            line = orders[place % 2]
+            latest = max([spot for spot, bit in enumerate(line) if away & bit], default=-1)
+            return (line[latest] if away else 0), line[latest + 1 :]
+        if away & 1:
+            return 1, []
+        return away, ([] if away else list(range(2, fibres, 2))) + [1]
+
+    def depth(step, away):
+        count = 0
+        while away:
+            away ^= route(step, away)[0]
+            count += 1
+        return count
+
+    def settle(step, away):
+        came, onward = route(step, away)
+        if came:
+            hop(step, away ^ came, came).wait_recv()
         elif step:
             swap_arrival(step).wait_recv()
-        for bit in line[latest + 1 :]:
+        for bit in onward:
             copy = hop(step, away, bit)
             copy.start()
             started.append(copy)
-    keep.wait()
+        block, window = lax.bitwise_xor(me, away), lax.bitwise_xor(win, step)
+        pltpu.make_async_copy(held_v.at[block, window], out_ref.at[block, window], keep_sem).start()
+
+    events = sorted(
+        (place + depth(step, away), place, depth(step, away & ~1), away, step)
+        for place, step in enumerate(turns) for away in range(fibres)
+    )
+    for turn, step in enumerate(turns):
+        if step:
+            target = lax.bitwise_xor(win, step)
+            whiten_group(target, white_v.at[target])
+            swap(step).start()
+        else:
+            whiten_group(win, held_v.at[me, win])
+        due = [event for event in events if event[0] + (2 if event[1] else 1 if event[3] else 0) <= turn]
+        events = [event for event in events if event not in due]
+        for _, _, _, away, due_step in due:
+            settle(due_step, away)
+    for _, _, _, away, step in events:
+        settle(step, away)
     for step in range(1, wins):
         swap(step).wait_send()
     for copy in started:
         copy.wait_send()
+    pltpu.make_async_copy(held_v, out_ref, keep_sem).wait()
 
 
 def stack_kernel(steps, scale, per_turn, plan_ref, gathered_ref, out_ref, blocks_v, left_v, right_v, result_v, load_sem, out_sem):
@@ -339,7 +360,7 @@
     margin, half_time = kernel.shape[0] // 2, kernel.shape[1] // 2
     bins = FB // wins
     halo = -(-margin // ROWS) * ROWS
-    assert own_windows == 1 and bins % BLK == 0 and fibres & (fibres - 1) == 0
+    assert own_windows == 1 and bins % BLK == 0 and fibres & (fibres - 1) == 0 and wins & (wins - 1) == 0
     table = transform_table(samples, bins, half_time)
     phases = phase_table(samples, half_time)
     any_space = pl.BlockSpec(memory_space=pl.ANY)
@@ -347,20 +368,22 @@
         functools.partial(spectra_kernel, fibres, wins, margin, half_time),
         out_shape=jax.ShapeDtypeStruct((fibres, wins, 2, bins, channels), jnp.bfloat16),
         in_specs=[
-            pl.BlockSpec(memory_space=pltpu.SMEM),
+            pl.BlockSpec(memory_space=pltpu.HBM),
             pl.BlockSpec(memory_space=pltpu.HBM),
             pl.BlockSpec(memory_space=pltpu.HBM),
             pl.BlockSpec(memory_space=pltpu.HBM),
         ],
         out_specs=any_space,
         scratch_shapes=[
+            pltpu.SMEM(kernel.shape, jnp.float32),
             pltpu.VMEM(phases.shape, jnp.float32),
             pltpu.VMEM(table.shape, jnp.bfloat16),
             pltpu.VMEM((channels + 2 * halo, samples), jnp.bfloat16),
             pltpu.VMEM((samples, channels + 2 * halo), jnp.bfloat16),
             pltpu.VMEM((channels + 2 * halo, kernel.shape[1] * channels), jnp.bfloat16),
             pltpu.VMEM((wins, 2, bins, channels), jnp.bfloat16),
-            pltpu.SemaphoreType.DMA((3,)),
+            pltpu.VMEM((fibres, wins, 2, bins, channels), jnp.bfloat16),
+            pltpu.SemaphoreType.DMA((4,)),
             pltpu.SemaphoreType.DMA((2,)),
             pltpu.SemaphoreType.DMA((2,)),
             pltpu.SemaphoreType.DMA((wins,)),

time: 45.5 us -> 40.7 us (0.89)
  Pallas kernels: 43.9 us -> 38.6 us
    pallas_call x1, Pallas kernels: 33.2 us -> 27.9 us  [shards(): pl.pallas_call(functools.partial(spectra_kernel, fibres, wins, margin, ha...]
where the time goes in v6:
time: 40.7 us; the launch traced here: 40 us
  Pallas kernels  38.6 us (95%)
  local copies, waits for them, and re-layouts  1.38 us (3%)
    pallas_call x1, Pallas kernels, shards(): pl.pallas_call(functools.partial(spectra_kernel, fibres, wins, margin, ha...  27.9 us
    pallas_call x1, Pallas kernels, shards(): pl.pallas_call(functools.partial(stack_kernel, steps, 1.0 / math.sqrt(win...  10.7 us
    convert_element_type x1, local copies, waits for them, and re-layouts, shards(): kernel.astype(jnp.float32)  1.38 us

profile of v6, /device:TPU:0, one launch (start us, length us, event | category | flops | bytes accessed | tf_op | source)
XLA Modules:
  0.0 40.0 jit_solution(4310216152821082444)
XLA Ops:
  0.0 1.4 %copy.7.taps_hbm = f32[31,9]{1,0:T(8,128)} copy(bf16[31,9]{0,1:T(8,128)(2,1)} %param.6) | data formatting | bytes 1674 | tf_op jit(solution)/shard_map/convert_element_type | solution.py:399
  1.4 27.9 %spectra.1.gathered_ref = bf16[8,4,2,64,128]{4,3,2,1,0:T(8,128)(2,1)} custom-call(f32[31,9]{1,0:T(8,128)} %copy.7.taps_hbm, f32[256,8]{1,0:T(8,128)} %constant.4.clone.phase_hbm, bf16[1088,2048]{1,0:T(8,128)(2,1)} %constant.5.clone.table_ref, bf16[128,2048]{1,0:T(8,128)(2,1)} %bitcast.1), custom_call_target="tpu_custom_call" | custom-call | tf_op jit(solution)/shard_map/spectra/pallas_call | solution.py:367
  29.3 10.7 %stacks.1 = bf16[4,64,2,128,128]{4,3,2,1,0:T(8,128)(2,1)} custom-call(s32[4]{0:T(128)} %plan_ref.1, bf16[8,4,2,64,128]{4,3,2,1,0:T(8,128)(2,1)} %spectra.1.gathered_ref), custom_call_target="tpu_custom_call" | custom-call | tf_op jit(solution)/shard_map/stacks/pallas_call | solution.py:403

commit v7 on v6

--- a/solution.py
+++ b/solution.py
@@ -57,7 +57,7 @@
 def spectra_kernel(
     fibres, wins, margin, half_time,
     taps_hbm, phase_hbm, table_ref, strain_ref, out_ref,
-    taps_ref, phase_ref, table_v, x_v, xt_v, band_v, white_v, held_v,
+    taps_v, taps_ref, phase_ref, table_v, x_v, xt_v, band_v, white_v, held_v,
     load_sem, halo_send, halo_recv, swap_send, swap_recv, keep_sem, gather_send, gather_recv,
 ):
     me = lax.axis_index("fibre")
@@ -74,7 +74,7 @@
     load_own.start()
     load_phase = pltpu.make_async_copy(phase_hbm, phase_ref, load_sem.at[2])
     load_phase.start()
-    load_taps = pltpu.make_async_copy(taps_hbm, taps_ref, load_sem.at[3])
+    load_taps = pltpu.make_async_copy(taps_hbm, taps_v, load_sem.at[3])
     load_taps.start()
 
     barrier = pltpu.get_barrier_semaphore()
@@ -122,6 +122,7 @@
     lax.fori_loop(0, x_v.shape[1] // 256, turn_over, 0)
 
     load_taps.wait()
+    taps_ref[...] = taps_v[...].astype(jnp.float32)
 
     def band_rows(first_row, rows, source):
         lag = source - lax.broadcasted_iota(jnp.int32, (rows, channels), 1) + margin
@@ -129,7 +130,8 @@
         for tap in range(chan_taps):
             here = lag == tap
             totals = [
-                jnp.where(here, taps_ref[tap, offset + half_time], total) for total, offset in zip(totals, order)
+                jnp.where(here, taps_ref[offset + half_time : offset + half_time + 1, tap : tap + 1], total)
+                for total, offset in zip(totals, order)
             ]
         for place, total in enumerate(totals):
             band_v[pl.ds(first_row, rows), place * channels : (place + 1) * channels] = total.astype(jnp.bfloat16)
@@ -235,7 +237,7 @@
 
     def route(step, away):
         place = turns.index(step)
-        if place < wins // 2:
+        if place == 0:
             line = orders[place % 2]
             latest = max([spot for spot, bit in enumerate(line) if away & bit], default=-1)
             return (line[latest] if away else 0), line[latest + 1 :]
@@ -375,7 +377,8 @@
         ],
         out_specs=any_space,
         scratch_shapes=[
-            pltpu.SMEM(kernel.shape, jnp.float32),
+            pltpu.VMEM(kernel.shape[::-1], kernel.dtype),
+            pltpu.VMEM(kernel.shape[::-1], jnp.float32),
             pltpu.VMEM(phases.shape, jnp.float32),
             pltpu.VMEM(table.shape, jnp.bfloat16),
             pltpu.VMEM((channels + 2 * halo, samples), jnp.bfloat16),
@@ -396,7 +399,7 @@
             collective_id=0, has_side_effects=True, vmem_limit_bytes=60 * 1024 * 1024
         ),
         name="spectra",
-    )(kernel.astype(jnp.float32), jnp.asarray(phases), jnp.asarray(table), strain.reshape(channels, samples))
+    )(kernel.T, jnp.asarray(phases), jnp.asarray(table), strain.reshape(channels, samples))
 
     steps = plan.shape[0]
     per_turn = 8

time: 40.7 us -> 40.3 us (level)
  local copies, waits for them, and re-layouts: 1.38 us -> 0 us
  Pallas kernels: 38.6 us -> 39.6 us
    convert_element_type x1 -> x0, local copies, waits for them, and re-layouts: 1.38 us -> none  [shards(): kernel.astype(jnp.float32)]
    pallas_call x1, Pallas kernels: 27.9 us -> 28.9 us  [shards(): pl.pallas_call(functools.partial(spectra_kernel, fibres, wins, margin, ha...]
where the time goes in v7:
time: 40.3 us; the launch traced here: 39.6 us
  Pallas kernels  39.6 us (98%)
    pallas_call x1, Pallas kernels, shards(): pl.pallas_call(functools.partial(spectra_kernel, fibres, wins, margin, ha...  28.9 us
    pallas_call x1, Pallas kernels, shards(): pl.pallas_call(functools.partial(stack_kernel, steps, 1.0 / math.sqrt(win...  10.7 us

profile of v7, /device:TPU:0, one launch (start us, length us, event | category | flops | bytes accessed | tf_op | source)
XLA Modules:
  0.0 39.6 jit_solution(3617486299771974052)
XLA Ops:
  0.0 28.9 %spectra.1.gathered_ref = bf16[8,4,2,64,128]{4,3,2,1,0:T(8,128)(2,1)} custom-call(bf16[9,31]{1,0:T(8,128)(2,1)} %bitcast.3, f32[256,8]{1,0:T(8,128)} %constant.4.clone.phase_hbm, bf16[1088,2048]{1,0:T(8,128)(2,1)} %constant.5.clone.table_ref, bf16[128,2048]{1,0:T(8,128)(2,1)} %bitcast.2), custom_call_target="tpu_custom_call" | custom-call | tf_op jit(solution)/shard_map/spectra/pallas_call | solution.py:369
  28.9 10.7 %stacks.1 = bf16[4,64,2,128,128]{4,3,2,1,0:T(8,128)(2,1)} custom-call(s32[4]{0:T(128)} %plan_ref.1, bf16[8,4,2,64,128]{4,3,2,1,0:T(8,128)(2,1)} %spectra.1.gathered_ref), custom_call_target="tpu_custom_call" | custom-call | tf_op jit(solution)/shard_map/stacks/pallas_call | solution.py:406
